TPU v7x, 256 devices: a whole 4x4x8 slice. The times are simulated.
256 devices in a mesh: wide: 16 (over x, y_lo, core), narrow: 16 (over y_hi, z).
Axes of the slice: x: 4, y: 4 (y_hi: 2, y_lo: 2; y = y_hi * 2 + y_lo), z: 8, core: 2. Of those that a mesh axis runs over, the one named last changes fastest.
Arguments:
- pose_feats: bfloat16 [16384, 1024], P(('wide', 'narrow')), may hold values from -3 to 3
- text_feats: bfloat16 [16384, 1024], P(('wide', 'narrow')), may hold values from -3 to 3
- match: int32 [16384], P(('wide', 'narrow')), may hold values from 0 to 16383, as said below
- pose_head: bfloat16 [1024, 1024], replicated, may hold values from -1 to 1
- text_head: bfloat16 [1024, 1024], replicated, may hold values from -1 to 1
Outputs:
- loss: float32 [], replicated
- grad_pose: float32 [16384, 1024], P(('wide', 'narrow'))
- grad_text: float32 [16384, 1024], P(('wide', 'narrow'))
- head_grads: float32 [1024, 2048], P('wide')
Inputs may be any that keep to these rules, and one draw needn't show every extreme that they name: `match`: every text index appears exactly once.
All inputs are finite; a program needn't handle non-finite values.
Results may differ from a plain program's by a relative error of at most 0.0049.
Values may be sent and summed in bfloat16 or wider, within the bound.
No kernel may reach another device: no remote copies, remote signals or barrier semaphores. Data moves between devices by JAX's collectives and lax.ppermute only.
A program may use at most 64 MiB of HBM per device.

v0:
```python
import functools
import math

import jax
import jax.numpy as jnp
from jax import lax
from jax.experimental import pallas as pl
from jax.experimental.pallas import tpu as pltpu
from jax.sharding import Mesh
from jax.sharding import PartitionSpec as P

epsilon = 1e-06
logit_bias = -10.0
log1p_terms = (
    0.9999997615814209,
    -0.49997174739837646,
    0.3327192962169647,
    -0.24474774301052094,
    0.1768747717142105,
    -0.1068500280380249,
    0.04349390044808388,
    -0.00837115291506052,
)

AXES = ("x", "yl", "core", "yh", "z")
PLANE = ("x", "yl", "yh")
LINE = ("core", "z")
NX, NY, NZ, NC = 4, 4, 8, 2
ROWS = 64
N = 1024
EXTRA = 128
TILE = 512
STEPS = N // TILE

NT = (((1,), (1,)), ((), ()))
TN = (((0,), (0,)), ((), ()))
NN = (((1,), (0,)), ((), ()))
TT = (((0,), (1,)), ((), ()))


def device_index(x, y, z, c):
    return (((x * 2 + y % 2) * 2 + c) * 2 + y // 2) * NZ + z


def pairs_of(move):
    out = []
    for x in range(NX):
        for y in range(NY):
            for z in range(NZ):
                for c in range(NC):
                    x2, y2, z2, c2 = move(x, y, z, c)
                    out.append(
                        (device_index(x, y, z, c), device_index(x2 % NX, y2 % NY, z2 % NZ, c2 % NC))
                    )
    return out


def send(value, move):
    return lax.ppermute(value, AXES, pairs_of(move))


def swap_cores(value):
    return send(value, lambda x, y, z, c: (x, y, z, 1 - c))


def ring_pieces(shard, move):
    half = shard.shape[0] // 2
    below = send(shard, move(1))
    above = send(shard, move(-1))
    far_low = send(below[:half], move(1))
    far_high = send(above[half:], move(-1))
    return ((shard, 0, 0), (below, 3, 0), (above, 1, 0), (far_low, 2, 0), (far_high, 2, half))


def plane_move(x_core):
    def move_by(by):
        def move(x, y, z, c):
            return (x + by, y, z, c) if c == x_core else (x, y + by, z, c)

        return move

    return move_by


def y_slot(y):
    return y % 2 * 2 + y // 2


def dot(a, b, dims):
    return lax.dot_general(a, b, dims, preferred_element_type=jnp.float32)


def inverse_norm(raw):
    return lax.rsqrt(jnp.sum(raw * raw, axis=0, keepdims=True) + epsilon)


def reciprocal(value):
    guess = pltpu.reciprocal(value, approx=True)
    return guess * (2.0 - value * guess)


def back_cols(grad, unit, inverse):
    inner = jnp.sum(unit * grad, axis=0, keepdims=True)
    return ((grad - unit * inner) * inverse).astype(jnp.bfloat16)


def cols(step):
    return slice(step * TILE, (step + 1) * TILE)


def pair_kernel(
    scale,
    grad_scale,
    near_hbm,
    below_hbm,
    above_hbm,
    far_low_hbm,
    far_high_hbm,
    pose_head_hbm,
    text_own_hbm,
    text_other_hbm,
    text_head_hbm,
    loss_ref,
    pose_rows_hbm,
    keep_hbm,
    give_hbm,
    pose_feats_ref,
    pose_head_ref,
    text_feats_ref,
    text_head_ref,
    pose_ref,
    pose_unit_ref,
    text_ref,
    text_unit_ref,
    weights_ref,
    text_back_ref,
    pose_back_ref,
    pose_rows_ref,
    pose_term_ref,
    in_sems,
    out_sems,
):
    second = lax.axis_index("core")
    out = []

    def fetch(source, target, number):
        copy = pltpu.make_async_copy(source, target, in_sems.at[number])
        copy.start()
        return copy

    def store(source, target):
        copy = pltpu.make_async_copy(source, target, out_sems.at[len(out)])
        copy.start()
        out.append(copy)

    def store_halves(source, kind, where):
        for half, target in ((second, keep_hbm), (1 - second, give_hbm)):
            for block in range(NZ):
                to = lax.rem(block + NZ - lax.axis_index("z"), NZ)
                store(source.at[half, block, :, where], target.at[to, kind, :, where])

    def split(value):
        return value.astype(jnp.bfloat16).reshape(2, 8, ROWS, value.shape[1])

    def half_rows(half):
        return pl.ds(pl.multiple_of(half * (N // 2), N // 2), N // 2)

    pose_head_in = fetch(pose_head_hbm, pose_head_ref, 0)
    pose_in = []
    x, y = lax.axis_index("x"), lax.axis_index("yh") * 2 + lax.axis_index("yl")
    for source, offset, first in (
        (near_hbm, 0, 0),
        (below_hbm, 3, 0),
        (above_hbm, 1, 0),
        (far_low_hbm, 2, 0),
        (far_high_hbm, 2, 2),
    ):
        x_at = lax.rem(x + offset, 4)
        y_at = lax.rem(y + offset, 4)
        y_at = lax.rem(y_at, 2) * 2 + y_at // 2
        for block in range(source.shape[0] // ROWS):
            place = jnp.where(second == 0, x_at * 4 + first + block, (first + block) * 4 + y_at)
            at = pl.multiple_of(place * ROWS, ROWS)
            pose_in.append(
                fetch(
                    source.at[block * ROWS : (block + 1) * ROWS, :],
                    pose_feats_ref.at[pl.ds(at, ROWS), :],
                    1 + len(pose_in),
                )
            )
    text_head_in = fetch(text_head_hbm, text_head_ref, 17)
    own_in = fetch(text_own_hbm, text_feats_ref.at[half_rows(second), :], 18)
    other_in = fetch(text_other_hbm, text_feats_ref.at[half_rows(1 - second), :], 19)

    pose_raws, text_raws = [], []
    pose_head_in.wait()
    for copy in pose_in:
        copy.wait()
    for step in range(STEPS):
        pose_raws.append(dot(pose_head_ref[...], pose_feats_ref[cols(step), :N], TT))
    text_head_in.wait()
    own_in.wait()
    other_in.wait()
    pose_inverses, text_inverses = [], []
    for step in range(STEPS):
        text_raws.append(dot(text_head_ref[...], text_feats_ref[cols(step), :], TT))
        pose_inverses.append(inverse_norm(pose_raws[step]))
        unit = pose_raws[step] * pose_inverses[step]
        pose_unit_ref[:, cols(step)] = unit
        pose_ref[:, cols(step)] = unit.astype(jnp.bfloat16)
    for step in range(STEPS):
        text_inverses.append(inverse_norm(text_raws[step]))
        unit = text_raws[step] * text_inverses[step]
        text_unit_ref[:, cols(step)] = unit
        text_ref[:, cols(step)] = unit.astype(jnp.bfloat16)

    lanes = lax.broadcasted_iota(jnp.int32, (8, EXTRA), 1)
    pick = jnp.where(lanes == 0, 128.0, jnp.where(lanes == 1, 1.0, 0.0)).astype(jnp.bfloat16)
    match = dot(pick, pose_feats_ref[:, N:], NT).astype(jnp.int32)[0:1, :]
    place = lax.axis_index("x") * 2 + lax.axis_index("yl")
    offset = match - (place * 2048 + lax.axis_index("yh") * 512)
    late = offset >= 1024
    within = jnp.where(late, offset - 1024, offset)
    inside = (within >= 0) & (within < 512)
    target = jnp.where(inside, within + jnp.where(late, 512, 0), -1)

    inner = [dot(text_ref[:, cols(0)], pose_ref[...], TN)]
    loss_sum = None
    text_grads = []
    for step in range(STEPS):
        if step + 1 < STEPS:
            inner.append(dot(text_ref[:, cols(step + 1)], pose_ref[...], TN))
        logits = scale * inner[step] + logit_bias
        ids = lax.broadcasted_iota(jnp.int32, (TILE, 1), 0) + step * TILE
        paired = ids == target
        positive = paired != (logits >= 0.0)
        size = jnp.abs(logits)
        small = jnp.exp(-size)
        sig = jnp.where(positive, 1.0, small) * reciprocal(1.0 + small)
        weights_ref[cols(step), :] = (jnp.where(paired, -grad_scale, grad_scale) * sig).astype(
            jnp.bfloat16
        )
        poly = jnp.full_like(small, log1p_terms[-1])
        for term in log1p_terms[-2::-1]:
            poly = poly * small + term
        loss = jnp.where(positive, size, 0.0) + small * poly
        part = jnp.sum(loss.reshape(TILE // 8, 8, N), axis=0)
        loss_sum = part if loss_sum is None else loss_sum + part
        text_grads.append(dot(pose_ref[...], weights_ref[cols(step), :], NT))
    loss_ref[...] = loss_sum

    pose_grads = [dot(text_ref[...], weights_ref[:, cols(0)], NN)]
    for step in range(STEPS):
        if step + 1 < STEPS:
            pose_grads.append(dot(text_ref[...], weights_ref[:, cols(step + 1)], NN))
        text_back_ref[:, :, :, cols(step)] = split(
            back_cols(text_grads[step], text_unit_ref[:, cols(step)], text_inverses[step])
        )
        store_halves(text_back_ref, 0, cols(step))
    for step in range(STEPS):
        back = back_cols(pose_grads[step], pose_unit_ref[:, cols(step)], pose_inverses[step])
        pose_back_ref[:, cols(step)] = back
    for step in range(STEPS):
        pose_term_ref[:, :, :, cols(step)] = split(
            dot(pose_back_ref[...], pose_feats_ref[:, cols(step)], NN)
        )
        store_halves(pose_term_ref, 1, cols(step))
        pose_rows_ref[cols(step), :] = pose_back_ref[:, cols(step)].T
        store(pose_rows_ref.at[cols(step), :], pose_rows_hbm.at[cols(step), :])
    for copy in out:
        copy.wait()


def loss_block(value):
    high = value.astype(jnp.bfloat16)
    rest = value - high.astype(jnp.float32)
    middle = rest.astype(jnp.bfloat16)
    low = (rest - middle.astype(jnp.float32)).astype(jnp.bfloat16)
    rows = lax.broadcasted_iota(jnp.int32, (16, 2 * ROWS), 0)
    block = jnp.where(
        rows == 0,
        high.astype(jnp.float32),
        jnp.where(
            rows == 1,
            middle.astype(jnp.float32),
            jnp.where(rows == 2, low.astype(jnp.float32), 0.0),
        ),
    )
    return block.astype(jnp.bfloat16)


def sum_loss(blocks):
    sums = jnp.sum(blocks.astype(jnp.float32), axis=0)
    return jnp.sum(sums[:3], axis=0, keepdims=True)


def terms_kernel(both_ref, own_ref, other_ref, loss_ref, out_ref):
    second = lax.axis_index("core")

    def text_cols(half):
        return both_ref[:ROWS, pl.ds(pl.multiple_of(half * (N // 2), N // 2), N // 2)]

    text_term = dot(text_cols(second), own_ref[...], NN)
    text_term += dot(text_cols(1 - second), other_ref[...], NN)
    text_term = text_term.astype(jnp.bfloat16)
    block = loss_block(jnp.full((16, 2 * ROWS), jnp.sum(loss_ref[...]), jnp.float32))
    for place in range(8):
        where = slice(place * 2 * ROWS, (place + 1) * 2 * ROWS)
        for high in range(2):
            out_ref[place * 2 + high, :ROWS, :] = both_ref[ROWS:, where]
            out_ref[place * 2 + high, ROWS : 2 * ROWS, :] = text_term[:, where]
            out_ref[place * 2 + high, 2 * ROWS :, :] = block


def turn_kernel(plane_ref, rows_ref, out_ref):
    sums = jnp.sum(plane_ref[:, : 2 * ROWS, :].astype(jnp.float32), axis=0).T.astype(jnp.bfloat16)
    total = sum_loss(plane_ref[:, 2 * ROWS :, :])
    block = loss_block(jnp.broadcast_to(total, (16, 2 * ROWS)))
    for core in range(NC):
        for z in range(NZ):
            out_ref[core * NZ + z, :ROWS, :] = sums[core * ROWS : (core + 1) * ROWS]
            out_ref[core * NZ + z, ROWS : ROWS + 32, :] = rows_ref[core * NZ + z]
            out_ref[core * NZ + z, ROWS + 32 :, :] = block


def last_kernel(line_ref, head_ref, grad_ref, heads_ref, loss_ref, text_ref):
    for m in range(16):
        text_ref[m * ROWS : m * ROWS + 32, :] = line_ref[m, ROWS : ROWS + 32, :ROWS]
        text_ref[m * ROWS + 32 : (m + 1) * ROWS, :] = line_ref[m, ROWS : ROWS + 32, ROWS:]
    grad_ref[...] = dot(text_ref[...], head_ref[...], TT)
    for m in range(0, 16, 2):
        for kind in range(2):
            lanes = slice(kind * ROWS, (kind + 1) * ROWS)
            pair = [line_ref[m + i, :ROWS, lanes].astype(jnp.float32) for i in range(2)]
            heads_ref[:, kind * N + m * ROWS : kind * N + (m + 2) * ROWS] = jnp.concatenate(
                pair, axis=1
            )
    total = sum_loss(line_ref[:, ROWS + 32 :, :]) / float(N * 16) ** 2
    loss_ref[...] = total[:, :1]


VMEM = pl.BlockSpec(memory_space=pltpu.VMEM)
ANY = pl.BlockSpec(memory_space=pl.ANY)


def shape(rows, dtype):
    return jax.ShapeDtypeStruct((rows, N), dtype)


def score(scale, grad_scale, pose_pieces, pose_head, text_own, text_other, text_head):
    half = pltpu.VMEM((N, N), jnp.bfloat16)
    full = pltpu.VMEM((N, N), jnp.float32)
    blocks = pltpu.VMEM((2, 8, ROWS, N), jnp.bfloat16)
    return pl.pallas_call(
        functools.partial(pair_kernel, scale, grad_scale),
        out_shape=(
            shape(8, jnp.float32),
            shape(N, jnp.bfloat16),
            jax.ShapeDtypeStruct((8, 2, ROWS, N), jnp.bfloat16),
            jax.ShapeDtypeStruct((8, 2, ROWS, N), jnp.bfloat16),
        ),
        in_specs=[ANY] * 9,
        out_specs=(VMEM, ANY, ANY, ANY),
        scratch_shapes=[
            pltpu.VMEM((N, N + EXTRA), jnp.bfloat16),
            half,
            half,
            half,
            half,
            full,
            half,
            full,
            half,
            blocks,
            half,
            half,
            blocks,
            pltpu.SemaphoreType.DMA((20,)),
            pltpu.SemaphoreType.DMA(((4 * NZ + 1) * STEPS,)),
        ],
        compiler_params=pltpu.CompilerParams(vmem_limit_bytes=58 * 1024 * 1024),
        cost_estimate=pl.CostEstimate(
            flops=12 * N**3, bytes_accessed=20 * N * N, transcendentals=2 * N * N
        ),
    )(*pose_pieces, pose_head, text_own, text_other, text_head)


def small_call(kernel, out_shape, scratch, *args):
    return pl.pallas_call(
        kernel,
        out_shape=out_shape,
        in_specs=[VMEM] * len(args),
        out_specs=jax.tree.map(lambda _: VMEM, out_shape),
        scratch_shapes=scratch,
        compiler_params=pltpu.CompilerParams(vmem_limit_bytes=16 * 1024 * 1024),
        cost_estimate=pl.CostEstimate(
            flops=2 * ROWS * N * N, bytes_accessed=4 * N * N, transcendentals=0
        ),
    )(*args)


def fold(blocks):
    return jnp.concatenate([blocks[:, : ROWS // 2], blocks[:, ROWS // 2 :]], axis=2)


def along_z(by):
    return lambda x, y, z, c: (x, y, z + by, c)


def ring_sum(keep, got):
    half = keep.shape[1] // 2

    def own(by):
        return keep[by % NZ].astype(jnp.float32) + got[by % NZ].astype(jnp.float32)

    def bf(value):
        return value.astype(jnp.bfloat16)

    up = send(bf(own(4)[:half]), along_z(1))
    down = send(bf(own(4)[half:]), along_z(-1))
    for by in (3, 2, 1):
        upper, lower = own(by), own(-by)
        if by == 3:
            up = jnp.concatenate([upper[:half] + up.astype(jnp.float32), upper[half:]])
            down = jnp.concatenate([lower[:half], lower[half:] + down.astype(jnp.float32)])
        else:
            up = upper + up.astype(jnp.float32)
            down = lower + down.astype(jnp.float32)
        up = send(bf(up), along_z(1))
        down = send(bf(down), along_z(-1))
    return bf(own(0) + up.astype(jnp.float32) + down.astype(jnp.float32))


def repeat_kernel(rows_hbm, out_hbm, sems):
    copies = [pltpu.make_async_copy(rows_hbm, out_hbm.at[b], sems.at[b]) for b in range(NZ)]
    for copy in copies:
        copy.start()
    for copy in copies:
        copy.wait()


def repeat(rows):
    return pl.pallas_call(
        repeat_kernel,
        out_shape=jax.ShapeDtypeStruct((NZ, *rows.shape), rows.dtype),
        in_specs=[ANY],
        out_specs=ANY,
        scratch_shapes=[pltpu.SemaphoreType.DMA((NZ,))],
        compiler_params=pltpu.CompilerParams(vmem_limit_bytes=1024 * 1024),
    )(rows)


def local(pose_feats, text_feats, match, pose_head, text_head):
    batch_size = ROWS * 256
    logit_scale = 2.0 * math.sqrt(N)
    grad_scale = logit_scale / math.sqrt(batch_size)
    x = lax.axis_index("x")
    y = lax.axis_index("yh") * 2 + lax.axis_index("yl")
    first = lax.axis_index("core") == 0

    text_own = lax.all_to_all(repeat(text_feats), "z", 0, 0)
    text_own = text_own.reshape(NZ * ROWS, N)
    ids = jnp.stack([match // 128, match % 128], axis=1).astype(jnp.bfloat16)
    shard = jnp.concatenate([pose_feats, jnp.pad(ids, ((0, 0), (0, EXTRA - 2)))], axis=1)
    column = jnp.zeros((4 * ROWS, N + EXTRA), jnp.bfloat16)
    for value, offset, start in ring_pieces(shard, plane_move(1)):
        place = jnp.where(first, y_slot((y + offset) % 4), (x + offset) % 4)
        column = lax.dynamic_update_slice(column, value, (place * ROWS + start, 0))
    pieces = [piece for piece, _, _ in ring_pieces(column, plane_move(0))]
    text_own, *pieces[3:] = lax.optimization_barrier((text_own, *pieces[3:]))
    text_other = swap_cores(text_own)

    loss_part, pose_part, keep, give = score(
        logit_scale, grad_scale, pieces, pose_head, text_own, text_other, text_head
    )
    got = swap_cores(give)
    pose_parts = lax.all_to_all(pose_part.reshape(16, ROWS, N), PLANE, 0, 0)
    both = ring_sum(keep.reshape(NZ, 2 * ROWS, N), got.reshape(NZ, 2 * ROWS, N))

    both, pose_parts = lax.optimization_barrier((both, pose_parts))
    pose_back = jnp.sum(pose_parts.astype(jnp.float32), axis=0).astype(jnp.bfloat16)
    grad_pose = dot(pose_back, pose_head, NT)

    bf16 = jnp.bfloat16
    terms = small_call(
        terms_kernel,
        jax.ShapeDtypeStruct((16, 2 * ROWS + 16, 2 * ROWS), bf16),
        [],
        both,
        text_own,
        text_other,
        loss_part,
    )
    plane = lax.all_to_all(terms, PLANE, 0, 0)
    text_rows = fold(both[:ROWS].reshape(ROWS, 16, ROWS).transpose(1, 0, 2))
    turned = small_call(
        turn_kernel,
        jax.ShapeDtypeStruct((16, ROWS + 48, 2 * ROWS), bf16),
        [],
        plane,
        text_rows,
    )
    line = lax.all_to_all(turned, LINE, 0, 0)
    grad_text, head_grads, loss = small_call(
        last_kernel,
        (
            shape(ROWS, jnp.float32),
            jax.ShapeDtypeStruct((ROWS, 2 * N), jnp.float32),
            jax.ShapeDtypeStruct((1, 1), jnp.float32),
        ),
        [pltpu.VMEM((N, ROWS), bf16)],
        line,
        text_head,
    )
    return (loss.reshape(()), grad_pose, grad_text, head_grads)


def solution(mesh):
    fine = Mesh(mesh.devices.reshape(NX, 2, NC, 2, NZ), AXES)
    placed = (P(AXES, None), P(AXES, None), P(AXES), P(), P())
    return jax.shard_map(
        local,
        mesh=fine,
        in_specs=placed,
        out_specs=(P(), P(AXES, None), P(AXES, None), P(("x", "yl", "core"), None)),
        check_vma=False,
    )
```

profile of v0, /device:TPU:32, one launch (start us, length us, event | category | flops | bytes accessed | tf_op | source)
XLA Modules:
  0.0 156.4 jit_solution(2604416495585026898)
XLA Ops:
  0.7 0.7 convert_bitcast_fusion
  1.4 0.1 copy.14
  1.5 0.9 fusion.11
  2.5 1.7 %collective-permute-start = (bf16[64,1152]{1,0:T(8,128)(2,1)S(1)}, bf16[64,1152]{1,0:T(8,128)(2,1)S(1)}, u32[]{:S(2)}, u32[]{:S(2)}) collective-permute-start(bf16[64,1152]{1,0:T(8,128)(2,1)S(1)} %get-tuple-element.40), channel_id=1, source_target_pairs={{0,32},{16,80},{1,33},{17,81},{2,34},{18,82},{3,35},{19,83},{4,36}... | collective-permute-start | bytes 442376 | tf_op jit(solution)/shard_map/ppermute | solution.py:59
  4.1 1.7 %collective-permute-start.1 = (bf16[64,1152]{1,0:T(8,128)(2,1)S(1)}, bf16[64,1152]{1,0:T(8,128)(2,1)S(1)}, u32[]{:S(2)}, u32[]{:S(2)}) collective-permute-start(bf16[64,1152]{1,0:T(8,128)(2,1)S(1)} %get-tuple-element.40), channel_id=1, source_target_pairs={{0,40},{16,208},{1,41},{17,209},{2,42},{18,210},{3,43},{19,211},{4... | collective-permute-start | bytes 442376 | tf_op jit(solution)/shard_map/ppermute | solution.py:59
  5.8 0.9 copy-done.5
  6.7 1.1 shard_map.84
  7.8 8.6 %all-to-all-start = ((bf16[8,64,1024]{2,1,0:T(8,128)(2,1)}), bf16[8,64,1024]{2,1,0:T(8,128)(2,1)S(1)}, u32[]{:S(2)}, u32[]{:S(2)}) async-start(bf16[8,64,1024]{2,1,0:T(8,128)(2,1)} %shard_map.84), calls=%async_computation | async-start | bytes 2097152 | tf_op jit(solution)/shard_map/all_to_all | solution.py:461
  16.4 0.0 collective-permute-done
  16.4 0.4 collective-permute-start.2
  16.8 0.0 collective-permute-done.1
  16.8 2.9 %collective-permute-start.3 = (bf16[32,1152]{1,0:T(8,128)(2,1)S(1)}, bf16[32,1152]{1,0:T(8,128)(2,1)S(1)}, u32[]{:S(2)}, u32[]{:S(2)}) collective-permute-start(bf16[32,1152]{1,0:T(8,128)(2,1)S(1)} %slice.157), channel_id=1, source_target_pairs={{0,40},{16,208},{1,41},{17,209},{2,42},{18,210},{3,43},{19,211},{4... | collective-permute-start | bytes 221192 | tf_op jit(solution)/shard_map/ppermute | solution.py:59
  19.8 2.2 %collective-permute-done.2 = bf16[32,1152]{1,0:T(8,128)(2,1)S(1)} collective-permute-done((bf16[32,1152]{1,0:T(8,128)(2,1)S(1)}, bf16[32,1152]{1,0:T(8,128)(2,1)S(1)}, u32[]{:S(2)}, u32[]{:S(2)}) %collective-permute-start.2) | collective-permute-done | bytes 73760 | tf_op jit(solution)/shard_map/ppermute | solution.py:59
  22.0 0.0 collective-permute-done.3
  22.1 2.8 %collective-permute-start.5 = (bf16[256,1152]{1,0:T(8,128)(2,1)S(1)}, bf16[256,1152]{1,0:T(8,128)(2,1)S(1)}, u32[]{:S(2)}, u32[]{:S(2)}) collective-permute-start(bf16[256,1152]{1,0:T(8,128)(2,1)S(1)} %constant_dynamic-update-slice_fusion.near_hbm), channel_id=1, source_target_pairs={{0,192},{16,56},{1,193},{17,57},{2,194},{18,58},{3,195},{19,59},{4... | collective-permute-start | bytes 1769480 | tf_op jit(solution)/shard_map/ppermute | solution.py:59
  24.9 0.0 collective-permute-start.4
  24.9 7.4 %collective-permute-done.5.above_hbm = bf16[256,1152]{1,0:T(8,128)(2,1)S(1)} collective-permute-done((bf16[256,1152]{1,0:T(8,128)(2,1)S(1)}, bf16[256,1152]{1,0:T(8,128)(2,1)S(1)}, u32[]{:S(2)}, u32[]{:S(2)}) %collective-permute-start.5) | collective-permute-done | bytes 589856 | tf_op jit(solution)/shard_map/ppermute | solution.py:59
  32.3 3.8 %collective-permute-start.7 = (bf16[128,1152]{1,0:T(8,128)(2,1)S(1)}, bf16[128,1152]{1,0:T(8,128)(2,1)S(1)}, u32[]{:S(2)}, u32[]{:S(2)}) collective-permute-start(bf16[128,1152]{1,0:T(8,128)(2,1)S(1)} %slice.159), channel_id=1, source_target_pairs={{0,192},{16,56},{1,193},{17,57},{2,194},{18,58},{3,195},{19,59},{4... | collective-permute-start | bytes 884744 | tf_op jit(solution)/shard_map/ppermute | solution.py:59
  36.1 0.0 collective-permute-done.4.below_hbm
  36.1 0.1 collective-permute-start.6
  36.2 4.1 %collective-permute-done.7.far_high_hbm = bf16[128,1152]{1,0:T(8,128)(2,1)S(1)} collective-permute-done((bf16[128,1152]{1,0:T(8,128)(2,1)S(1)}, bf16[128,1152]{1,0:T(8,128)(2,1)S(1)}, u32[]{:S(2)}, u32[]{:S(2)}) %collective-permute-start.7) | collective-permute-done | bytes 294944 | tf_op jit(solution)/shard_map/ppermute | solution.py:59
  40.3 3.8 %collective-permute-done.6.far_low_hbm = bf16[128,1152]{1,0:T(8,128)(2,1)S(1)} collective-permute-done((bf16[128,1152]{1,0:T(8,128)(2,1)S(1)}, bf16[128,1152]{1,0:T(8,128)(2,1)S(1)}, u32[]{:S(2)}, u32[]{:S(2)}) %collective-permute-start.6) | collective-permute-done | bytes 294944 | tf_op jit(solution)/shard_map/ppermute | solution.py:59
  44.1 0.0 all-to-all-done
  44.2 0.3 collective-permute-start.8
  44.4 2.6 %collective-permute-done.8.text_other_hbm.other_ref = bf16[512,1024]{1,0:T(8,128)(2,1)S(1)} collective-permute-done((bf16[512,1024]{1,0:T(8,128)(2,1)S(1)}, bf16[512,1024]{1,0:T(8,128)(2,1)S(1)}, u32[]{:S(2)}, u32[]{:S(2)}) %collective-permute-start.8) | collective-permute-done | bytes 1048608 | tf_op jit(solution)/shard_map/ppermute | solution.py:59
  47.1 1.0 copy-done.3
  48.1 23.3 %shard_map.85 = (f32[8,1024]{1,0:T(8,128)}, bf16[1024,1024]{1,0:T(8,128)(2,1)}, bf16[8,2,64,1024]{3,2,1,0:T(8,128)(2,1)}, bf16[8,2,64,1024]{3,2,1,0:T(8,128)(2,1)}) custom-call(bf16[256,1152]{1,0:T(8,128)(2,1)} %copy-done.8, bf16[256,1152]{1,0:T(8,128)(2,1)} %copy-done.10, bf16[256,1152]{1,0:T(8,128)(2,1)} %copy-done.9, bf16[128,1152]{1,0:T(8,128)(2,1)} %copy-done.12, ...), custom_call_target="tpu_custom_call" | custom-call | flops 12884901888 | bytes 20971520 | tf_op jit(solution)/shard_map/pallas_call | solution.py:354
  71.4 0.2 collective-permute-start.9
  71.6 4.9 %all-to-all-start.1 = ((bf16[16,64,1024]{2,1,0:T(8,128)(2,1)}), bf16[16,64,1024]{2,1,0:T(8,128)(2,1)}, u32[]{:S(2)}, u32[]{:S(2)}) async-start(bf16[16,64,1024]{2,1,0:T(8,128)(2,1)} %bitcast.57), calls=%async_computation.1 | async-start | bytes 4194304 | tf_op jit(solution)/shard_map/all_to_all | solution.py:477
  76.5 2.4 %convert_add_fusion.3 = (f32[1,2,64,1024]{3,2,1,0:T(8,128)S(1)}, f32[1,2,64,1024]{3,2,1,0:T(8,128)S(1)}, f32[1,2,64,1024]{3,2,1,0:T(8,128)S(1)}, f32[1,2,64,1024...) fusion(bf16[8,2,64,1024]{3,2,1,0:T(8,128)(2,1)} %collective-per, ...), kind=kLoop, calls=%fused_computation.15 | loop fusion | flops 3276800 | bytes 8126464 | tf_op jit(solution)/shard_map/add | solution.py:414
  79.0 1.6 collective-permute-start.10
  80.6 0.5 collective-permute-start.14
  81.1 4.7 %collective-permute-done.14 = bf16[64,1024]{1,0:T(8,128)(2,1)S(1)} collective-permute-done((bf16[64,1024]{1,0:T(8,128)(2,1)S(1)}, bf16[64,1024]{1,0:T(8,128)(2,1)S(1)}, u32[]{:S(2)}, u32[]{:S(2)}) %collective-permute-start.14) | collective-permute-done | bytes 131104 | tf_op jit(solution)/shard_map/ppermute | solution.py:59
  85.8 0.6 collective-permute-start.15
  86.5 0.0 collective-permute-done.10
  86.5 1.9 %collective-permute-start.11 = (bf16[128,1024]{1,0:T(8,128)(2,1)S(1)}, bf16[128,1024]{1,0:T(8,128)(2,1)S(1)}, u32[]{:S(2)}, u32[]{:S(2)}) collective-permute-start(bf16[128,1024]{1,0:T(8,128)(2,1)S(1)} %pad_maximum_fusion), channel_id=1, source_target_pairs={{0,1},{16,17},{1,2},{17,18},{2,3},{18,19},{3,4},{19,20},{4,5},{20,... | collective-permute-start | bytes 786440 | tf_op jit(solution)/shard_map/ppermute | solution.py:59
  88.4 5.7 %collective-permute-done.15 = bf16[128,1024]{1,0:T(8,128)(2,1)S(1)} collective-permute-done((bf16[128,1024]{1,0:T(8,128)(2,1)S(1)}, bf16[128,1024]{1,0:T(8,128)(2,1)S(1)}, u32[]{:S(2)}, u32[]{:S(2)}) %collective-permute-start.15) | collective-permute-done | bytes 262176 | tf_op jit(solution)/shard_map/ppermute | solution.py:59
  94.1 0.1 fusion
  94.2 0.9 collective-permute-start.16
  95.0 0.5 collective-permute-done.11
  95.5 0.1 fusion.2
  95.6 1.5 collective-permute-start.12
  97.1 4.8 %collective-permute-done.16 = bf16[128,1024]{1,0:T(8,128)(2,1)S(1)} collective-permute-done((bf16[128,1024]{1,0:T(8,128)(2,1)S(1)}, bf16[128,1024]{1,0:T(8,128)(2,1)S(1)}, u32[]{:S(2)}, u32[]{:S(2)}) %collective-permute-start.16) | collective-permute-done | bytes 262176 | tf_op jit(solution)/shard_map/ppermute | solution.py:59
  101.8 0.1 fusion.1
  101.9 0.9 collective-permute-start.17
  102.8 0.5 collective-permute-done.12
  103.3 0.1 fusion.3
  103.4 1.7 %collective-permute-start.13 = (bf16[128,1024]{1,0:T(8,128)(2,1)S(1)}, bf16[128,1024]{1,0:T(8,128)(2,1)S(1)}, u32[]{:S(2)}, u32[]{:S(2)}) collective-permute-start(bf16[128,1024]{1,0:T(8,128)(2,1)S(1)} %fusion.3), channel_id=1, source_target_pairs={{0,1},{16,17},{1,2},{17,18},{2,3},{18,19},{3,4},{19,20},{4,5},{20,... | collective-permute-start | bytes 786440 | tf_op jit(solution)/shard_map/ppermute | solution.py:59
  105.0 3.9 %collective-permute-done.17 = bf16[128,1024]{1,0:T(8,128)(2,1)S(1)} collective-permute-done((bf16[128,1024]{1,0:T(8,128)(2,1)S(1)}, bf16[128,1024]{1,0:T(8,128)(2,1)S(1)}, u32[]{:S(2)}, u32[]{:S(2)}) %collective-permute-start.17) | collective-permute-done | bytes 262176 | tf_op jit(solution)/shard_map/ppermute | solution.py:59
  108.9 2.3 %collective-permute-done.13 = bf16[128,1024]{1,0:T(8,128)(2,1)S(1)} collective-permute-done((bf16[128,1024]{1,0:T(8,128)(2,1)S(1)}, bf16[128,1024]{1,0:T(8,128)(2,1)S(1)}, u32[]{:S(2)}, u32[]{:S(2)}) %collective-permute-start.13) | collective-permute-done | bytes 262176 | tf_op jit(solution)/shard_map/ppermute | solution.py:59
  111.3 0.1 fusion.5.both_ref
  111.4 0.9 all-to-all-done.1
  112.3 1.3 shard_map.86
  113.6 5.7 %all-to-all-start.2 = ((bf16[16,144,128]{2,1,0:T(8,128)(2,1)}), bf16[16,144,128]{2,1,0:T(8,128)(2,1)S(1)}, u32[]{:S(2)}, u32[]{:S(2)}) async-start(bf16[16,144,128]{2,1,0:T(8,128)(2,1)} %shard_map.86), calls=%async_computation.2 | async-start | bytes 1179648 | tf_op jit(solution)/shard_map/all_to_all | solution.py:494
  119.3 0.2 reshape.90
  119.5 0.1 copy.17
  119.6 0.1 pad_maximum_fusion.2.rows_ref
  119.7 10.2 %all-to-all-done.2.plane_ref = bf16[16,144,128]{2,1,0:T(8,128)(2,1)S(1)} async-done(((bf16[16,144,128]{2,1,0:T(8,128)(2,1)}), bf16[16,144,128]{2,1,0:T(8,128)(2,1)S(1)}, u32[]{:S(2)}, u32[]{:S(2)}) %all-to-all-start.2) | async-done | bytes 589856 | tf_op jit(solution)/shard_map/all_to_all | solution.py:494
  129.9 0.9 shard_map.87
  130.9 8.8 %all-to-all-start.3 = ((bf16[16,112,128]{2,1,0:T(8,128)(2,1)}), bf16[16,112,128]{2,1,0:T(8,128)(2,1)S(1)}, u32[]{:S(2)}, u32[]{:S(2)}) async-start(bf16[16,112,128]{2,1,0:T(8,128)(2,1)} %shard_map.87), calls=%async_computation.3 | async-start | bytes 917504 | tf_op jit(solution)/shard_map/all_to_all | solution.py:503
  139.7 2.1 %reduce_sum.12 = bf16[64,1024]{1,0:T(8,128)(2,1)S(1)} reduce(bf16[16,64,1024]{2,1,0:T(8,128)(2,1)} %all-to-all-done.1, bf16[]{:T(256)} %constant.144.clone.1), dimensions={0}, to_apply=%region_0.1 | reduce | flops 983040 | bytes 2228226 | tf_op jit(solution)/shard_map/reduce_sum | solution.py:481
  141.8 3.1 %fusion.17 = f32[64,1024]{1,0:T(8,128)} fusion(bf16[64,1024]{1,0:T(8,128)(2,1)S(1)} %reduce_sum.12, bf16[1024,1024]{1,0:T(8,128)(2,1)} %pose_head_hbm.1), kind=kOutput, calls=%fused_computation.53 | convolution fusion | flops 134217728 | bytes 2490368 | tf_op jit(solution)/shard_map/dot_general | solution.py:90
  144.9 9.8 %all-to-all-done.3.line_ref = bf16[16,112,128]{2,1,0:T(8,128)(2,1)S(1)} async-done(((bf16[16,112,128]{2,1,0:T(8,128)(2,1)}), bf16[16,112,128]{2,1,0:T(8,128)(2,1)S(1)}, u32[]{:S(2)}, u32[]{:S(2)}) %all-to-all-start.3) | async-done | bytes 458784 | tf_op jit(solution)/shard_map/all_to_all | solution.py:503
  154.7 1.7 %shard_map.88 = (f32[64,1024]{1,0:T(8,128)}, f32[64,2048]{1,0:T(8,128)}, f32[1,1]{1,0:T(1,128)}) custom-call(bf16[16,112,128]{2,1,0:T(8,128)(2,1)S(1)} %all-to-all-done.3.line_ref, bf16[1024,1024]{1,0:T(8,128)(2,1)S(1)} %copy-done.2), custom_call_target="tpu_custom_call" | custom-call | flops 134217728 | bytes 4194304 | tf_op jit(solution)/shard_map/pallas_call | solution.py:389
  (44 shorter events, 0.4 us)
Async XLA Ops:
  2.5 13.9 %collective-permute-start = (bf16[64,1152]{1,0:T(8,128)(2,1)S(1)}, bf16[64,1152]{1,0:T(8,128)(2,1)S(1)}, u32[]{:S(2)}, u32[]{:S(2)}) collective-permute-start(bf16[64,1152]{1,0:T(8,128)(2,1)S(1)} %get-tuple-element.40), channel_id=1, source_target_pairs={{0,32},{16,80},{1,33},{17,81},{2,34},{18,82},{3,35},{19,83},{4,36}... | collective-permute-start | bytes 442376 | tf_op jit(solution)/shard_map/ppermute | solution.py:59
  4.1 12.7 %collective-permute-start.1 = (bf16[64,1152]{1,0:T(8,128)(2,1)S(1)}, bf16[64,1152]{1,0:T(8,128)(2,1)S(1)}, u32[]{:S(2)}, u32[]{:S(2)}) collective-permute-start(bf16[64,1152]{1,0:T(8,128)(2,1)S(1)} %get-tuple-element.40), channel_id=1, source_target_pairs={{0,40},{16,208},{1,41},{17,209},{2,42},{18,210},{3,43},{19,211},{4... | collective-permute-start | bytes 442376 | tf_op jit(solution)/shard_map/ppermute | solution.py:59
  5.8 0.9 copy-start.5
  7.8 36.4 %all-to-all-start = ((bf16[8,64,1024]{2,1,0:T(8,128)(2,1)}), bf16[8,64,1024]{2,1,0:T(8,128)(2,1)S(1)}, u32[]{:S(2)}, u32[]{:S(2)}) async-start(bf16[8,64,1024]{2,1,0:T(8,128)(2,1)} %shard_map.84), calls=%async_computation | async-start | bytes 2097152 | tf_op jit(solution)/shard_map/all_to_all | solution.py:461
  16.4 5.6 %collective-permute-start.2 = (bf16[32,1152]{1,0:T(8,128)(2,1)S(1)}, bf16[32,1152]{1,0:T(8,128)(2,1)S(1)}, u32[]{:S(2)}, u32[]{:S(2)}) collective-permute-start(bf16[32,1152]{1,0:T(8,128)(2,1)S(1)} %slice.156), channel_id=1, source_target_pairs={{0,32},{16,80},{1,33},{17,81},{2,34},{18,82},{3,35},{19,83},{4,36}... | collective-permute-start | bytes 221192 | tf_op jit(solution)/shard_map/ppermute | solution.py:59
  16.8 5.2 %collective-permute-start.3 = (bf16[32,1152]{1,0:T(8,128)(2,1)S(1)}, bf16[32,1152]{1,0:T(8,128)(2,1)S(1)}, u32[]{:S(2)}, u32[]{:S(2)}) collective-permute-start(bf16[32,1152]{1,0:T(8,128)(2,1)S(1)} %slice.157), channel_id=1, source_target_pairs={{0,40},{16,208},{1,41},{17,209},{2,42},{18,210},{3,43},{19,211},{4... | collective-permute-start | bytes 221192 | tf_op jit(solution)/shard_map/ppermute | solution.py:59
  22.1 25.0 %copy-start.8 = (bf16[256,1152]{1,0:T(8,128)(2,1)}, bf16[256,1152]{1,0:T(8,128)(2,1)S(1)}, u32[]{:S(2)}) copy-start(bf16[256,1152]{1,0:T(8,128)(2,1)S(1)} %constant_dynamic-update-slice_fusion.near_hbm) | copy-start | bytes 1769476
  22.1 10.2 %collective-permute-start.5 = (bf16[256,1152]{1,0:T(8,128)(2,1)S(1)}, bf16[256,1152]{1,0:T(8,128)(2,1)S(1)}, u32[]{:S(2)}, u32[]{:S(2)}) collective-permute-start(bf16[256,1152]{1,0:T(8,128)(2,1)S(1)} %constant_dynamic-update-slice_fusion.near_hbm), channel_id=1, source_target_pairs={{0,192},{16,56},{1,193},{17,57},{2,194},{18,58},{3,195},{19,59},{4... | collective-permute-start | bytes 1769480 | tf_op jit(solution)/shard_map/ppermute | solution.py:59
  24.9 11.2 %collective-permute-start.4 = (bf16[256,1152]{1,0:T(8,128)(2,1)S(1)}, bf16[256,1152]{1,0:T(8,128)(2,1)S(1)}, u32[]{:S(2)}, u32[]{:S(2)}) collective-permute-start(bf16[256,1152]{1,0:T(8,128)(2,1)S(1)} %constant_dynamic-update-slice_fusion.near_hbm), channel_id=1, source_target_pairs={{0,64},{16,48},{1,65},{17,49},{2,66},{18,50},{3,67},{19,51},{4,68}... | collective-permute-start | bytes 1769480 | tf_op jit(solution)/shard_map/ppermute | solution.py:59
  32.3 14.8 %copy-start.9 = (bf16[256,1152]{1,0:T(8,128)(2,1)}, bf16[256,1152]{1,0:T(8,128)(2,1)S(1)}, u32[]{:S(2)}) copy-start(bf16[256,1152]{1,0:T(8,128)(2,1)S(1)} %collective-permute-done.5.above_hbm) | copy-start | bytes 1769476
  32.3 8.0 %collective-permute-start.7 = (bf16[128,1152]{1,0:T(8,128)(2,1)S(1)}, bf16[128,1152]{1,0:T(8,128)(2,1)S(1)}, u32[]{:S(2)}, u32[]{:S(2)}) collective-permute-start(bf16[128,1152]{1,0:T(8,128)(2,1)S(1)} %slice.159), channel_id=1, source_target_pairs={{0,192},{16,56},{1,193},{17,57},{2,194},{18,58},{3,195},{19,59},{4... | collective-permute-start | bytes 884744 | tf_op jit(solution)/shard_map/ppermute | solution.py:59
  36.1 11.0 %copy-start.10 = (bf16[256,1152]{1,0:T(8,128)(2,1)}, bf16[256,1152]{1,0:T(8,128)(2,1)S(1)}, u32[]{:S(2)}) copy-start(bf16[256,1152]{1,0:T(8,128)(2,1)S(1)} %collective-permute-done.4.below_hbm) | copy-start | bytes 1769476
  36.1 8.0 %collective-permute-start.6 = (bf16[128,1152]{1,0:T(8,128)(2,1)S(1)}, bf16[128,1152]{1,0:T(8,128)(2,1)S(1)}, u32[]{:S(2)}, u32[]{:S(2)}) collective-permute-start(bf16[128,1152]{1,0:T(8,128)(2,1)S(1)} %slice.158), channel_id=1, source_target_pairs={{0,64},{16,48},{1,65},{17,49},{2,66},{18,50},{3,67},{19,51},{4,68}... | collective-permute-start | bytes 884744 | tf_op jit(solution)/shard_map/ppermute | solution.py:59
  40.3 6.7 %copy-start.11 = (bf16[128,1152]{1,0:T(8,128)(2,1)}, bf16[128,1152]{1,0:T(8,128)(2,1)S(1)}, u32[]{:S(2)}) copy-start(bf16[128,1152]{1,0:T(8,128)(2,1)S(1)} %collective-permute-done.7.far_high_hbm) | copy-start | bytes 884740
  44.1 3.0 %copy-start.12 = (bf16[128,1152]{1,0:T(8,128)(2,1)}, bf16[128,1152]{1,0:T(8,128)(2,1)S(1)}, u32[]{:S(2)}) copy-start(bf16[128,1152]{1,0:T(8,128)(2,1)S(1)} %collective-permute-done.6.far_low_hbm) | copy-start | bytes 884740
  44.1 3.0 %copy-start = (bf16[8,64,1024]{2,1,0:T(8,128)(2,1)}, bf16[8,64,1024]{2,1,0:T(8,128)(2,1)S(1)}, u32[]{:S(2)}) copy-start(bf16[8,64,1024]{2,1,0:T(8,128)(2,1)S(1)} %all-to-all-done) | copy-start | bytes 3145732
  44.2 2.9 %collective-permute-start.8 = (bf16[512,1024]{1,0:T(8,128)(2,1)S(1)}, bf16[512,1024]{1,0:T(8,128)(2,1)S(1)}, u32[]{:S(2)}, u32[]{:S(2)}) collective-permute-start(bf16[512,1024]{1,0:T(8,128)(2,1)S(1)} %bitcast.54), channel_id=1, source_target_pairs={{0,16},{16,0},{1,17},{17,1},{2,18},{18,2},{3,19},{19,3},{4,20},{20... | collective-permute-start | bytes 3145736 | tf_op jit(solution)/shard_map/ppermute | solution.py:59
  47.1 1.0 copy-start.3
  71.4 5.1 %collective-permute-start.9 = (bf16[8,2,64,1024]{3,2,1,0:T(8,128)(2,1)}, bf16[8,2,64,1024]{3,2,1,0:T(8,128)(2,1)}, u32[]{:S(2)}, u32[]{:S(2)}) collective-permute-start(bf16[8,2,64,1024]{3,2,1,0:T(8,128)(2,1)} %get-tuple-element.20), channel_id=1, source_target_pairs={{0,16},{16,0},{1,17},{17,1},{2,18},{18,2},{3,19},{19,3},{4,20},{20... | collective-permute-start | bytes 6291464 | tf_op jit(solution)/shard_map/ppermute | solution.py:59
  71.6 4.9 %copy-start.7 = (bf16[8,2,64,1024]{3,2,1,0:T(8,128)(2,1)S(1)}, bf16[8,2,64,1024]{3,2,1,0:T(8,128)(2,1)}, u32[]{:S(2)}) copy-start(bf16[8,2,64,1024]{3,2,1,0:T(8,128)(2,1)} %get-tuple-element.19) | copy-start | bytes 6291460
  71.6 40.6 %all-to-all-start.1 = ((bf16[16,64,1024]{2,1,0:T(8,128)(2,1)}), bf16[16,64,1024]{2,1,0:T(8,128)(2,1)}, u32[]{:S(2)}, u32[]{:S(2)}) async-start(bf16[16,64,1024]{2,1,0:T(8,128)(2,1)} %bitcast.57), calls=%async_computation.1 | async-start | bytes 4194304 | tf_op jit(solution)/shard_map/all_to_all | solution.py:477
  79.0 7.5 %collective-permute-start.10 = (bf16[64,1024]{1,0:T(8,128)(2,1)S(1)}, bf16[64,1024]{1,0:T(8,128)(2,1)S(1)}, u32[]{:S(2)}, u32[]{:S(2)}) collective-permute-start(bf16[64,1024]{1,0:T(8,128)(2,1)S(1)} %get-tuple-element.38), channel_id=1, source_target_pairs={{0,1},{16,17},{1,2},{17,18},{2,3},{18,19},{3,4},{19,20},{4,5},{20,... | collective-permute-start | bytes 393224 | tf_op jit(solution)/shard_map/ppermute | solution.py:59
  80.6 5.2 %collective-permute-start.14 = (bf16[64,1024]{1,0:T(8,128)(2,1)S(1)}, bf16[64,1024]{1,0:T(8,128)(2,1)S(1)}, u32[]{:S(2)}, u32[]{:S(2)}) collective-permute-start(bf16[64,1024]{1,0:T(8,128)(2,1)S(1)} %get-tuple-element.39), channel_id=1, source_target_pairs={{0,7},{16,23},{1,0},{17,16},{2,1},{18,17},{3,2},{19,18},{4,3},{20,... | collective-permute-start | bytes 393224 | tf_op jit(solution)/shard_map/ppermute | solution.py:59
  85.8 8.3 %collective-permute-start.15 = (bf16[128,1024]{1,0:T(8,128)(2,1)S(1)}, bf16[128,1024]{1,0:T(8,128)(2,1)S(1)}, u32[]{:S(2)}, u32[]{:S(2)}) collective-permute-start(bf16[128,1024]{1,0:T(8,128)(2,1)S(1)} %pad_maximum_fusion.1), channel_id=1, source_target_pairs={{0,7},{16,23},{1,0},{17,16},{2,1},{18,17},{3,2},{19,18},{4,3},{20,... | collective-permute-start | bytes 786440 | tf_op jit(solution)/shard_map/ppermute | solution.py:59
  86.5 9.0 %collective-permute-start.11 = (bf16[128,1024]{1,0:T(8,128)(2,1)S(1)}, bf16[128,1024]{1,0:T(8,128)(2,1)S(1)}, u32[]{:S(2)}, u32[]{:S(2)}) collective-permute-start(bf16[128,1024]{1,0:T(8,128)(2,1)S(1)} %pad_maximum_fusion), channel_id=1, source_target_pairs={{0,1},{16,17},{1,2},{17,18},{2,3},{18,19},{3,4},{19,20},{4,5},{20,... | collective-permute-start | bytes 786440 | tf_op jit(solution)/shard_map/ppermute | solution.py:59
  94.2 7.7 %collective-permute-start.16 = (bf16[128,1024]{1,0:T(8,128)(2,1)S(1)}, bf16[128,1024]{1,0:T(8,128)(2,1)S(1)}, u32[]{:S(2)}, u32[]{:S(2)}) collective-permute-start(bf16[128,1024]{1,0:T(8,128)(2,1)S(1)} %fusion), channel_id=1, source_target_pairs={{0,7},{16,23},{1,0},{17,16},{2,1},{18,17},{3,2},{19,18},{4,3},{20,... | collective-permute-start | bytes 786440 | tf_op jit(solution)/shard_map/ppermute | solution.py:59
  95.5 16.8 %copy-start.1 = (bf16[8,64,1024]{2,1,0:T(8,128)(2,1)S(1)}, bf16[8,64,1024]{2,1,0:T(8,128)(2,1)}, u32[]{:S(2)}) copy-start(bf16[8,64,1024]{2,1,0:T(8,128)(2,1)} %copy-done) | copy-start | bytes 3145732
  95.5 16.8 %copy-start.4 = (bf16[512,1024]{1,0:T(8,128)(2,1)S(1)}, bf16[512,1024]{1,0:T(8,128)(2,1)}, u32[]{:S(2)}) copy-start(bf16[512,1024]{1,0:T(8,128)(2,1)} %copy-done.3) | copy-start | bytes 3145732
  95.5 16.8 %copy-start.6 = (f32[8,1024]{1,0:T(8,128)S(1)}, f32[8,1024]{1,0:T(8,128)}, u32[]{:S(2)}) copy-start(f32[8,1024]{1,0:T(8,128)} %get-tuple-element.23.loss_ref) | copy-start | bytes 98308
  95.6 7.7 %collective-permute-start.12 = (bf16[128,1024]{1,0:T(8,128)(2,1)S(1)}, bf16[128,1024]{1,0:T(8,128)(2,1)S(1)}, u32[]{:S(2)}, u32[]{:S(2)}) collective-permute-start(bf16[128,1024]{1,0:T(8,128)(2,1)S(1)} %fusion.2), channel_id=1, source_target_pairs={{0,1},{16,17},{1,2},{17,18},{2,3},{18,19},{3,4},{19,20},{4,5},{20,... | collective-permute-start | bytes 786440 | tf_op jit(solution)/shard_map/ppermute | solution.py:59
  101.9 7.0 %collective-permute-start.17 = (bf16[128,1024]{1,0:T(8,128)(2,1)S(1)}, bf16[128,1024]{1,0:T(8,128)(2,1)S(1)}, u32[]{:S(2)}, u32[]{:S(2)}) collective-permute-start(bf16[128,1024]{1,0:T(8,128)(2,1)S(1)} %fusion.1), channel_id=1, source_target_pairs={{0,7},{16,23},{1,0},{17,16},{2,1},{18,17},{3,2},{19,18},{4,3},{20,... | collective-permute-start | bytes 786440 | tf_op jit(solution)/shard_map/ppermute | solution.py:59
  103.4 7.9 %collective-permute-start.13 = (bf16[128,1024]{1,0:T(8,128)(2,1)S(1)}, bf16[128,1024]{1,0:T(8,128)(2,1)S(1)}, u32[]{:S(2)}, u32[]{:S(2)}) collective-permute-start(bf16[128,1024]{1,0:T(8,128)(2,1)S(1)} %fusion.3), channel_id=1, source_target_pairs={{0,1},{16,17},{1,2},{17,18},{2,3},{18,19},{3,4},{19,20},{4,5},{20,... | collective-permute-start | bytes 786440 | tf_op jit(solution)/shard_map/ppermute | solution.py:59
  113.6 16.4 %all-to-all-start.2 = ((bf16[16,144,128]{2,1,0:T(8,128)(2,1)}), bf16[16,144,128]{2,1,0:T(8,128)(2,1)S(1)}, u32[]{:S(2)}, u32[]{:S(2)}) async-start(bf16[16,144,128]{2,1,0:T(8,128)(2,1)} %shard_map.86), calls=%async_computation.2 | async-start | bytes 1179648 | tf_op jit(solution)/shard_map/all_to_all | solution.py:494
  130.9 23.8 %all-to-all-start.3 = ((bf16[16,112,128]{2,1,0:T(8,128)(2,1)}), bf16[16,112,128]{2,1,0:T(8,128)(2,1)S(1)}, u32[]{:S(2)}, u32[]{:S(2)}) async-start(bf16[16,112,128]{2,1,0:T(8,128)(2,1)} %shard_map.87), calls=%async_computation.3 | async-start | bytes 917504 | tf_op jit(solution)/shard_map/all_to_all | solution.py:503
  139.6 15.1 %copy-start.2 = (bf16[1024,1024]{1,0:T(8,128)(2,1)S(1)}, bf16[1024,1024]{1,0:T(8,128)(2,1)}, u32[]{:S(2)}) copy-start(bf16[1024,1024]{1,0:T(8,128)(2,1)} %head_ref.1) | copy-start | bytes 6291460
where the time goes:
time: 157 us; the launch traced here: 156 us
  waiting for transfers between devices  63.3 us (40%)
  starting transfers between devices  51.4 us (33%)
  Pallas kernels  28.3 us (18%)
  other arithmetic  6.76 us (4%)
  matrix products  3.06 us (2%)
  local copies, waits for them, and re-layouts  2.57 us (2%)
    ppermute x18, waiting for transfers between devices, send(): return lax.ppermute(value, AXES, pairs_of(move))  42.4 us
    ppermute x18, starting transfers between devices, send(): return lax.ppermute(value, AXES, pairs_of(move))  23.5 us
    pallas_call x1, Pallas kernels, score(): pl.pallas_call(functools.partial(pair_kernel, scale, grad_scale), out_sha...  23.3 us
    all_to_all x1, waiting for transfers between devices, local(): plane = lax.all_to_all(terms, PLANE, 0, 0)  10.2 us
    all_to_all x1, waiting for transfers between devices, local(): line = lax.all_to_all(turned, LINE, 0, 0)  9.84 us
    all_to_all x1, starting transfers between devices, local(): line = lax.all_to_all(turned, LINE, 0, 0)  8.79 us
    all_to_all x1, starting transfers between devices, local(): text_own = lax.all_to_all(repeat(text_feats), 'z', 0, 0)  8.58 us
    all_to_all x1, starting transfers between devices, local(): plane = lax.all_to_all(terms, PLANE, 0, 0)  5.72 us
  transfers between devices with their start and end apart: 22, of which 15 were waited for; matrix products, arithmetic and copies ran while one was open for 6% of the time, Pallas kernels for 1%

commit v1 on v0

--- a/solution.py
+++ b/solution.py
@@ -124,6 +124,8 @@
     pose_rows_hbm,
     keep_hbm,
     give_hbm,
+    keep_far_hbm,
+    give_far_hbm,
     pose_feats_ref,
     pose_head_ref,
     text_feats_ref,
@@ -154,10 +156,17 @@
         out.append(copy)
 
     def store_halves(source, kind, where):
-        for half, target in ((second, keep_hbm), (1 - second, give_hbm)):
-            for block in range(NZ):
-                to = lax.rem(block + NZ - lax.axis_index("z"), NZ)
-                store(source.at[half, block, :, where], target.at[to, kind, :, where])
+        for half, target in (
+            (second, (keep_hbm, keep_far_hbm)),
+            (1 - second, (give_hbm, give_far_hbm)),
+        ):
+            for by in range(NZ):
+                block = lax.rem(lax.axis_index("z") + by, NZ)
+                if by == NZ // 2:
+                    to = target[1].at[kind, :, where]
+                else:
+                    to = target[0].at[by - by // (NZ // 2 + 1), kind, :, where]
+                store(source.at[half, block, :, where], to)
 
     def split(value):
         return value.astype(jnp.bfloat16).reshape(2, 8, ROWS, value.shape[1])
@@ -356,11 +365,13 @@
         out_shape=(
             shape(8, jnp.float32),
             shape(N, jnp.bfloat16),
-            jax.ShapeDtypeStruct((8, 2, ROWS, N), jnp.bfloat16),
-            jax.ShapeDtypeStruct((8, 2, ROWS, N), jnp.bfloat16),
+            jax.ShapeDtypeStruct((7, 2, ROWS, N), jnp.bfloat16),
+            jax.ShapeDtypeStruct((7, 2, ROWS, N), jnp.bfloat16),
+            jax.ShapeDtypeStruct((2, ROWS, N), jnp.bfloat16),
+            jax.ShapeDtypeStruct((2, ROWS, N), jnp.bfloat16),
         ),
         in_specs=[ANY] * 9,
-        out_specs=(VMEM, ANY, ANY, ANY),
+        out_specs=(VMEM,) + (ANY,) * 5,
         scratch_shapes=[
             pltpu.VMEM((N, N + EXTRA), jnp.bfloat16),
             half,
@@ -407,17 +418,18 @@
     return lambda x, y, z, c: (x, y, z + by, c)
 
 
-def ring_sum(keep, got):
+def ring_sum(keep, got, keep_far, got_far):
     half = keep.shape[1] // 2
 
     def own(by):
-        return keep[by % NZ].astype(jnp.float32) + got[by % NZ].astype(jnp.float32)
+        at = by if by >= 0 else by + 7
+        return keep[at].astype(jnp.float32) + got[at].astype(jnp.float32)
 
     def bf(value):
         return value.astype(jnp.bfloat16)
 
-    up = send(bf(own(4)[:half]), along_z(1))
-    down = send(bf(own(4)[half:]), along_z(-1))
+    up = send(bf(keep_far[0].astype(jnp.float32) + got_far[0].astype(jnp.float32)), along_z(1))
+    down = send(bf(keep_far[1].astype(jnp.float32) + got_far[1].astype(jnp.float32)), along_z(-1))
     for by in (3, 2, 1):
         upper, lower = own(by), own(-by)
         if by == 3:
@@ -470,12 +482,15 @@
     text_own, *pieces[3:] = lax.optimization_barrier((text_own, *pieces[3:]))
     text_other = swap_cores(text_own)
 
-    loss_part, pose_part, keep, give = score(
+    loss_part, pose_part, keep, give, keep_far, give_far = score(
         logit_scale, grad_scale, pieces, pose_head, text_own, text_other, text_head
     )
+    got_far = swap_cores(give_far)
     got = swap_cores(give)
     pose_parts = lax.all_to_all(pose_part.reshape(16, ROWS, N), PLANE, 0, 0)
-    both = ring_sum(keep.reshape(NZ, 2 * ROWS, N), got.reshape(NZ, 2 * ROWS, N))
+    both = ring_sum(
+        keep.reshape(7, 2 * ROWS, N), got.reshape(7, 2 * ROWS, N), keep_far, got_far
+    )
 
     both, pose_parts = lax.optimization_barrier((both, pose_parts))
     pose_back = jnp.sum(pose_parts.astype(jnp.float32), axis=0).astype(jnp.bfloat16)

time: 157 us -> 155 us (0.987)
  waiting for transfers between devices: 63.3 us -> 61.1 us
    ppermute x18 -> x19, waiting for transfers between devices: 42.4 us -> 39.6 us  [send(): return lax.ppermute(value, AXES, pairs_of(move))]
    ppermute x18 -> x19, starting transfers between devices: 23.5 us -> 24.1 us  [send(): return lax.ppermute(value, AXES, pairs_of(move))]
  transfers between devices with their start and end apart: 22 -> 23, of which waited for: 15 -> 15; matrix products, arithmetic and copies ran while one was open for 6% -> 5% of each run, Pallas kernels for 1% -> 1%
where the time goes in v1:
time: 155 us; the launch traced here: 154 us
  waiting for transfers between devices  61.1 us (39%)
  starting transfers between devices  51.8 us (33%)
  Pallas kernels  28.2 us (18%)
  other arithmetic  6.52 us (4%)
  matrix products  3.06 us (2%)
  local copies, waits for them, and re-layouts  2.53 us (2%)
    ppermute x19, waiting for transfers between devices, send(): return lax.ppermute(value, AXES, pairs_of(move))  39.6 us
    ppermute x19, starting transfers between devices, send(): return lax.ppermute(value, AXES, pairs_of(move))  24.1 us
    pallas_call x1, Pallas kernels, score(): pl.pallas_call(functools.partial(pair_kernel, scale, grad_scale), out_sha...  23.2 us
    all_to_all x1, waiting for transfers between devices, local(): plane = lax.all_to_all(terms, PLANE, 0, 0)  10.6 us
    all_to_all x1, waiting for transfers between devices, local(): line = lax.all_to_all(turned, LINE, 0, 0)  9.84 us
    all_to_all x1, starting transfers between devices, local(): text_own = lax.all_to_all(repeat(text_feats), 'z', 0, 0)  8.58 us
    all_to_all x1, starting transfers between devices, local(): line = lax.all_to_all(turned, LINE, 0, 0)  8.39 us
    all_to_all x1, starting transfers between devices, local(): plane = lax.all_to_all(terms, PLANE, 0, 0)  5.93 us
  transfers between devices with their start and end apart: 23, of which 15 were waited for; matrix products, arithmetic and copies ran while one was open for 5% of the time, Pallas kernels for 1%

profile of v1, /device:TPU:32, one launch (start us, length us, event | category | flops | bytes accessed | tf_op | source)
XLA Modules:
  0.0 154.3 jit_solution(14490322844359862046)
XLA Ops:
  0.7 0.7 convert_bitcast_fusion
  1.4 0.1 copy.14
  1.5 0.9 fusion.11
  2.5 1.7 %collective-permute-start = (bf16[64,1152]{1,0:T(8,128)(2,1)S(1)}, bf16[64,1152]{1,0:T(8,128)(2,1)S(1)}, u32[]{:S(2)}, u32[]{:S(2)}) collective-permute-start(bf16[64,1152]{1,0:T(8,128)(2,1)S(1)} %get-tuple-element.43), channel_id=1, source_target_pairs={{0,32},{16,80},{1,33},{17,81},{2,34},{18,82},{3,35},{19,83},{4,36}... | collective-permute-start | bytes 442376 | tf_op jit(solution)/shard_map/ppermute | solution.py:59
  4.1 1.7 %collective-permute-start.1 = (bf16[64,1152]{1,0:T(8,128)(2,1)S(1)}, bf16[64,1152]{1,0:T(8,128)(2,1)S(1)}, u32[]{:S(2)}, u32[]{:S(2)}) collective-permute-start(bf16[64,1152]{1,0:T(8,128)(2,1)S(1)} %get-tuple-element.43), channel_id=1, source_target_pairs={{0,40},{16,208},{1,41},{17,209},{2,42},{18,210},{3,43},{19,211},{4... | collective-permute-start | bytes 442376 | tf_op jit(solution)/shard_map/ppermute | solution.py:59
  5.8 0.9 copy-done.5
  6.7 1.1 shard_map.84
  7.8 8.6 %all-to-all-start = ((bf16[8,64,1024]{2,1,0:T(8,128)(2,1)}), bf16[8,64,1024]{2,1,0:T(8,128)(2,1)S(1)}, u32[]{:S(2)}, u32[]{:S(2)}) async-start(bf16[8,64,1024]{2,1,0:T(8,128)(2,1)} %shard_map.84), calls=%async_computation | async-start | bytes 2097152 | tf_op jit(solution)/shard_map/all_to_all | solution.py:473
  16.4 0.0 collective-permute-done
  16.4 0.4 collective-permute-start.2
  16.8 0.0 collective-permute-done.1
  16.8 2.9 %collective-permute-start.3 = (bf16[32,1152]{1,0:T(8,128)(2,1)S(1)}, bf16[32,1152]{1,0:T(8,128)(2,1)S(1)}, u32[]{:S(2)}, u32[]{:S(2)}) collective-permute-start(bf16[32,1152]{1,0:T(8,128)(2,1)S(1)} %slice.149), channel_id=1, source_target_pairs={{0,40},{16,208},{1,41},{17,209},{2,42},{18,210},{3,43},{19,211},{4... | collective-permute-start | bytes 221192 | tf_op jit(solution)/shard_map/ppermute | solution.py:59
  19.8 2.2 %collective-permute-done.2 = bf16[32,1152]{1,0:T(8,128)(2,1)S(1)} collective-permute-done((bf16[32,1152]{1,0:T(8,128)(2,1)S(1)}, bf16[32,1152]{1,0:T(8,128)(2,1)S(1)}, u32[]{:S(2)}, u32[]{:S(2)}) %collective-permute-start.2) | collective-permute-done | bytes 73760 | tf_op jit(solution)/shard_map/ppermute | solution.py:59
  22.0 0.0 collective-permute-done.3
  22.1 2.8 %collective-permute-start.5 = (bf16[256,1152]{1,0:T(8,128)(2,1)S(1)}, bf16[256,1152]{1,0:T(8,128)(2,1)S(1)}, u32[]{:S(2)}, u32[]{:S(2)}) collective-permute-start(bf16[256,1152]{1,0:T(8,128)(2,1)S(1)} %constant_dynamic-update-slice_fusion.near_hbm), channel_id=1, source_target_pairs={{0,192},{16,56},{1,193},{17,57},{2,194},{18,58},{3,195},{19,59},{4... | collective-permute-start | bytes 1769480 | tf_op jit(solution)/shard_map/ppermute | solution.py:59
  24.9 0.0 collective-permute-start.4
  24.9 7.4 %collective-permute-done.5.above_hbm = bf16[256,1152]{1,0:T(8,128)(2,1)S(1)} collective-permute-done((bf16[256,1152]{1,0:T(8,128)(2,1)S(1)}, bf16[256,1152]{1,0:T(8,128)(2,1)S(1)}, u32[]{:S(2)}, u32[]{:S(2)}) %collective-permute-start.5) | collective-permute-done | bytes 589856 | tf_op jit(solution)/shard_map/ppermute | solution.py:59
  32.3 3.8 %collective-permute-start.7 = (bf16[128,1152]{1,0:T(8,128)(2,1)S(1)}, bf16[128,1152]{1,0:T(8,128)(2,1)S(1)}, u32[]{:S(2)}, u32[]{:S(2)}) collective-permute-start(bf16[128,1152]{1,0:T(8,128)(2,1)S(1)} %slice.151), channel_id=1, source_target_pairs={{0,192},{16,56},{1,193},{17,57},{2,194},{18,58},{3,195},{19,59},{4... | collective-permute-start | bytes 884744 | tf_op jit(solution)/shard_map/ppermute | solution.py:59
  36.1 0.0 collective-permute-done.4.below_hbm
  36.1 0.1 collective-permute-start.6
  36.2 4.1 %collective-permute-done.7.far_high_hbm = bf16[128,1152]{1,0:T(8,128)(2,1)S(1)} collective-permute-done((bf16[128,1152]{1,0:T(8,128)(2,1)S(1)}, bf16[128,1152]{1,0:T(8,128)(2,1)S(1)}, u32[]{:S(2)}, u32[]{:S(2)}) %collective-permute-start.7) | collective-permute-done | bytes 294944 | tf_op jit(solution)/shard_map/ppermute | solution.py:59
  40.4 3.8 %collective-permute-done.6.far_low_hbm = bf16[128,1152]{1,0:T(8,128)(2,1)S(1)} collective-permute-done((bf16[128,1152]{1,0:T(8,128)(2,1)S(1)}, bf16[128,1152]{1,0:T(8,128)(2,1)S(1)}, u32[]{:S(2)}, u32[]{:S(2)}) %collective-permute-start.6) | collective-permute-done | bytes 294944 | tf_op jit(solution)/shard_map/ppermute | solution.py:59
  44.2 0.3 collective-permute-start.8
  44.4 2.6 %collective-permute-done.8.text_other_hbm.other_ref = bf16[512,1024]{1,0:T(8,128)(2,1)S(1)} collective-permute-done((bf16[512,1024]{1,0:T(8,128)(2,1)S(1)}, bf16[512,1024]{1,0:T(8,128)(2,1)S(1)}, u32[]{:S(2)}, u32[]{:S(2)}) %collective-permute-start.8) | collective-permute-done | bytes 1048608 | tf_op jit(solution)/shard_map/ppermute | solution.py:59
  47.1 1.0 copy-done.3
  48.1 23.2 %shard_map.85 = (f32[8,1024]{1,0:T(8,128)}, bf16[1024,1024]{1,0:T(8,128)(2,1)}, bf16[7,2,64,1024]{3,2,1,0:T(8,128)(2,1)}, bf16[7,2,64,1024]{3,2,1,0:T(8,128)(2,1...) custom-call(bf16[256,1152]{1,0:T(8,128)(2,1)} %copy-done.8, bf16[256,1152]{1,0:T(8,128)(2,1)} %copy-done.11, ...), custom_call_target="tpu_custom_call" | custom-call | flops 12884901888 | bytes 20971520 | tf_op jit(solution)/shard_map/pallas_call | solution.py:363
  71.3 0.2 collective-permute-start.9
  71.5 0.4 collective-permute-start.10
  71.9 4.9 %all-to-all-start.1 = ((bf16[16,64,1024]{2,1,0:T(8,128)(2,1)}), bf16[16,64,1024]{2,1,0:T(8,128)(2,1)}, u32[]{:S(2)}, u32[]{:S(2)}) async-start(bf16[16,64,1024]{2,1,0:T(8,128)(2,1)} %bitcast.57), calls=%async_computation.1 | async-start | bytes 4194304 | tf_op jit(solution)/shard_map/all_to_all | solution.py:490
  76.8 0.1 fusion.12
  76.9 1.5 collective-permute-start.11
  78.4 0.6 collective-permute-start.15
  79.0 2.1 %convert_add_fusion.3 = (f32[1,2,64,1024]{3,2,1,0:T(8,128)S(1)}, f32[1,2,64,1024]{3,2,1,0:T(8,128)S(1)}, f32[1,2,64,1024]{3,2,1,0:T(8,128)S(1)}, f32[1,2,64,1024...) fusion(bf16[7,2,64,1024]{3,2,1,0:T(8,128)(2,1)} %collective-per, ...), kind=kLoop, calls=%fused_computation.14 | loop fusion | flops 2752512 | bytes 7340032 | tf_op jit(solution)/shard_map/add | solution.py:426
  81.1 2.3 %collective-permute-done.15 = bf16[64,1024]{1,0:T(8,128)(2,1)S(1)} collective-permute-done((bf16[64,1024]{1,0:T(8,128)(2,1)S(1)}, bf16[64,1024]{1,0:T(8,128)(2,1)S(1)}, u32[]{:S(2)}, u32[]{:S(2)}) %collective-permute-start.15) | collective-permute-done | bytes 131104 | tf_op jit(solution)/shard_map/ppermute | solution.py:59
  83.5 0.7 collective-permute-start.16
  84.2 1.9 %collective-permute-start.12 = (bf16[128,1024]{1,0:T(8,128)(2,1)S(1)}, bf16[128,1024]{1,0:T(8,128)(2,1)S(1)}, u32[]{:S(2)}, u32[]{:S(2)}) collective-permute-start(bf16[128,1024]{1,0:T(8,128)(2,1)S(1)} %pad_maximum_fusion), channel_id=1, source_target_pairs={{0,1},{16,17},{1,2},{17,18},{2,3},{18,19},{3,4},{19,20},{4,5},{20,... | collective-permute-start | bytes 786440 | tf_op jit(solution)/shard_map/ppermute | solution.py:59
  86.1 5.4 %collective-permute-done.16 = bf16[128,1024]{1,0:T(8,128)(2,1)S(1)} collective-permute-done((bf16[128,1024]{1,0:T(8,128)(2,1)S(1)}, bf16[128,1024]{1,0:T(8,128)(2,1)S(1)}, u32[]{:S(2)}, u32[]{:S(2)}) %collective-permute-start.16) | collective-permute-done | bytes 262176 | tf_op jit(solution)/shard_map/ppermute | solution.py:59
  91.5 0.1 fusion
  91.6 0.9 collective-permute-start.17
  92.5 0.5 collective-permute-done.12
  93.0 0.1 fusion.2
  93.0 1.5 collective-permute-start.13
  94.5 4.4 %collective-permute-done.17 = bf16[128,1024]{1,0:T(8,128)(2,1)S(1)} collective-permute-done((bf16[128,1024]{1,0:T(8,128)(2,1)S(1)}, bf16[128,1024]{1,0:T(8,128)(2,1)S(1)}, u32[]{:S(2)}, u32[]{:S(2)}) %collective-permute-start.17) | collective-permute-done | bytes 262176 | tf_op jit(solution)/shard_map/ppermute | solution.py:59
  99.0 0.1 fusion.1
  99.0 1.2 collective-permute-start.18
  100.2 0.5 collective-permute-done.13
  100.7 0.1 fusion.3
  100.8 1.6 %collective-permute-start.14 = (bf16[128,1024]{1,0:T(8,128)(2,1)S(1)}, bf16[128,1024]{1,0:T(8,128)(2,1)S(1)}, u32[]{:S(2)}, u32[]{:S(2)}) collective-permute-start(bf16[128,1024]{1,0:T(8,128)(2,1)S(1)} %fusion.3), channel_id=1, source_target_pairs={{0,1},{16,17},{1,2},{17,18},{2,3},{18,19},{3,4},{19,20},{4,5},{20,... | collective-permute-start | bytes 786440 | tf_op jit(solution)/shard_map/ppermute | solution.py:59
  102.3 3.9 %collective-permute-done.18 = bf16[128,1024]{1,0:T(8,128)(2,1)S(1)} collective-permute-done((bf16[128,1024]{1,0:T(8,128)(2,1)S(1)}, bf16[128,1024]{1,0:T(8,128)(2,1)S(1)}, u32[]{:S(2)}, u32[]{:S(2)}) %collective-permute-start.18) | collective-permute-done | bytes 262176 | tf_op jit(solution)/shard_map/ppermute | solution.py:59
  106.3 2.4 %collective-permute-done.14 = bf16[128,1024]{1,0:T(8,128)(2,1)S(1)} collective-permute-done((bf16[128,1024]{1,0:T(8,128)(2,1)S(1)}, bf16[128,1024]{1,0:T(8,128)(2,1)S(1)}, u32[]{:S(2)}, u32[]{:S(2)}) %collective-permute-start.14) | collective-permute-done | bytes 262176 | tf_op jit(solution)/shard_map/ppermute | solution.py:59
  108.7 0.1 fusion.5.both_ref
  108.8 1.0 all-to-all-done.1
  109.9 1.3 shard_map.86
  111.2 5.9 %all-to-all-start.2 = ((bf16[16,144,128]{2,1,0:T(8,128)(2,1)}), bf16[16,144,128]{2,1,0:T(8,128)(2,1)S(1)}, u32[]{:S(2)}, u32[]{:S(2)}) async-start(bf16[16,144,128]{2,1,0:T(8,128)(2,1)} %shard_map.86), calls=%async_computation.2 | async-start | bytes 1179648 | tf_op jit(solution)/shard_map/all_to_all | solution.py:509
  117.1 0.2 reshape.87
  117.3 0.1 copy.17
  117.4 0.1 pad_maximum_fusion.2.rows_ref
  117.5 10.6 %all-to-all-done.2.plane_ref = bf16[16,144,128]{2,1,0:T(8,128)(2,1)S(1)} async-done(((bf16[16,144,128]{2,1,0:T(8,128)(2,1)}), bf16[16,144,128]{2,1,0:T(8,128)(2,1)S(1)}, u32[]{:S(2)}, u32[]{:S(2)}) %all-to-all-start.2) | async-done | bytes 589856 | tf_op jit(solution)/shard_map/all_to_all | solution.py:509
  128.2 0.9 shard_map.87
  129.1 8.4 %all-to-all-start.3 = ((bf16[16,112,128]{2,1,0:T(8,128)(2,1)}), bf16[16,112,128]{2,1,0:T(8,128)(2,1)S(1)}, u32[]{:S(2)}, u32[]{:S(2)}) async-start(bf16[16,112,128]{2,1,0:T(8,128)(2,1)} %shard_map.87), calls=%async_computation.3 | async-start | bytes 917504 | tf_op jit(solution)/shard_map/all_to_all | solution.py:518
  137.5 2.1 %reduce_sum.12 = bf16[64,1024]{1,0:T(8,128)(2,1)S(1)} reduce(bf16[16,64,1024]{2,1,0:T(8,128)(2,1)} %all-to-all-done.1, bf16[]{:T(256)} %constant.144.clone.1), dimensions={0}, to_apply=%region_0.1 | reduce | flops 983040 | bytes 2228226 | tf_op jit(solution)/shard_map/reduce_sum | solution.py:496
  139.6 3.1 %fusion.19 = f32[64,1024]{1,0:T(8,128)} fusion(bf16[64,1024]{1,0:T(8,128)(2,1)S(1)} %reduce_sum.12, bf16[1024,1024]{1,0:T(8,128)(2,1)} %pose_head_hbm.1), kind=kOutput, calls=%fused_computation.54 | convolution fusion | flops 134217728 | bytes 2490368 | tf_op jit(solution)/shard_map/dot_general | solution.py:90
  142.7 9.8 %all-to-all-done.3.line_ref = bf16[16,112,128]{2,1,0:T(8,128)(2,1)S(1)} async-done(((bf16[16,112,128]{2,1,0:T(8,128)(2,1)}), bf16[16,112,128]{2,1,0:T(8,128)(2,1)S(1)}, u32[]{:S(2)}, u32[]{:S(2)}) %all-to-all-start.3) | async-done | bytes 458784 | tf_op jit(solution)/shard_map/all_to_all | solution.py:518
  152.6 1.7 %shard_map.88 = (f32[64,1024]{1,0:T(8,128)}, f32[64,2048]{1,0:T(8,128)}, f32[1,1]{1,0:T(1,128)}) custom-call(bf16[16,112,128]{2,1,0:T(8,128)(2,1)S(1)} %all-to-all-done.3.line_ref, bf16[1024,1024]{1,0:T(8,128)(2,1)S(1)} %copy-done.2), custom_call_target="tpu_custom_call" | custom-call | flops 134217728 | bytes 4194304 | tf_op jit(solution)/shard_map/pallas_call | solution.py:400
  (48 shorter events, 0.4 us)
Async XLA Ops:
  2.5 13.9 %collective-permute-start = (bf16[64,1152]{1,0:T(8,128)(2,1)S(1)}, bf16[64,1152]{1,0:T(8,128)(2,1)S(1)}, u32[]{:S(2)}, u32[]{:S(2)}) collective-permute-start(bf16[64,1152]{1,0:T(8,128)(2,1)S(1)} %get-tuple-element.43), channel_id=1, source_target_pairs={{0,32},{16,80},{1,33},{17,81},{2,34},{18,82},{3,35},{19,83},{4,36}... | collective-permute-start | bytes 442376 | tf_op jit(solution)/shard_map/ppermute | solution.py:59
  4.1 12.7 %collective-permute-start.1 = (bf16[64,1152]{1,0:T(8,128)(2,1)S(1)}, bf16[64,1152]{1,0:T(8,128)(2,1)S(1)}, u32[]{:S(2)}, u32[]{:S(2)}) collective-permute-start(bf16[64,1152]{1,0:T(8,128)(2,1)S(1)} %get-tuple-element.43), channel_id=1, source_target_pairs={{0,40},{16,208},{1,41},{17,209},{2,42},{18,210},{3,43},{19,211},{4... | collective-permute-start | bytes 442376 | tf_op jit(solution)/shard_map/ppermute | solution.py:59
  5.8 0.9 copy-start.5
  7.8 36.4 %all-to-all-start = ((bf16[8,64,1024]{2,1,0:T(8,128)(2,1)}), bf16[8,64,1024]{2,1,0:T(8,128)(2,1)S(1)}, u32[]{:S(2)}, u32[]{:S(2)}) async-start(bf16[8,64,1024]{2,1,0:T(8,128)(2,1)} %shard_map.84), calls=%async_computation | async-start | bytes 2097152 | tf_op jit(solution)/shard_map/all_to_all | solution.py:473
  16.4 5.6 %collective-permute-start.2 = (bf16[32,1152]{1,0:T(8,128)(2,1)S(1)}, bf16[32,1152]{1,0:T(8,128)(2,1)S(1)}, u32[]{:S(2)}, u32[]{:S(2)}) collective-permute-start(bf16[32,1152]{1,0:T(8,128)(2,1)S(1)} %slice.148), channel_id=1, source_target_pairs={{0,32},{16,80},{1,33},{17,81},{2,34},{18,82},{3,35},{19,83},{4,36}... | collective-permute-start | bytes 221192 | tf_op jit(solution)/shard_map/ppermute | solution.py:59
  16.8 5.2 %collective-permute-start.3 = (bf16[32,1152]{1,0:T(8,128)(2,1)S(1)}, bf16[32,1152]{1,0:T(8,128)(2,1)S(1)}, u32[]{:S(2)}, u32[]{:S(2)}) collective-permute-start(bf16[32,1152]{1,0:T(8,128)(2,1)S(1)} %slice.149), channel_id=1, source_target_pairs={{0,40},{16,208},{1,41},{17,209},{2,42},{18,210},{3,43},{19,211},{4... | collective-permute-start | bytes 221192 | tf_op jit(solution)/shard_map/ppermute | solution.py:59
  22.1 25.0 %copy-start.8 = (bf16[256,1152]{1,0:T(8,128)(2,1)}, bf16[256,1152]{1,0:T(8,128)(2,1)S(1)}, u32[]{:S(2)}) copy-start(bf16[256,1152]{1,0:T(8,128)(2,1)S(1)} %constant_dynamic-update-slice_fusion.near_hbm) | copy-start | bytes 1769476
  22.1 10.2 %collective-permute-start.5 = (bf16[256,1152]{1,0:T(8,128)(2,1)S(1)}, bf16[256,1152]{1,0:T(8,128)(2,1)S(1)}, u32[]{:S(2)}, u32[]{:S(2)}) collective-permute-start(bf16[256,1152]{1,0:T(8,128)(2,1)S(1)} %constant_dynamic-update-slice_fusion.near_hbm), channel_id=1, source_target_pairs={{0,192},{16,56},{1,193},{17,57},{2,194},{18,58},{3,195},{19,59},{4... | collective-permute-start | bytes 1769480 | tf_op jit(solution)/shard_map/ppermute | solution.py:59
  24.9 11.2 %collective-permute-start.4 = (bf16[256,1152]{1,0:T(8,128)(2,1)S(1)}, bf16[256,1152]{1,0:T(8,128)(2,1)S(1)}, u32[]{:S(2)}, u32[]{:S(2)}) collective-permute-start(bf16[256,1152]{1,0:T(8,128)(2,1)S(1)} %constant_dynamic-update-slice_fusion.near_hbm), channel_id=1, source_target_pairs={{0,64},{16,48},{1,65},{17,49},{2,66},{18,50},{3,67},{19,51},{4,68}... | collective-permute-start | bytes 1769480 | tf_op jit(solution)/shard_map/ppermute | solution.py:59
  32.3 14.8 %copy-start.10 = (bf16[256,1152]{1,0:T(8,128)(2,1)}, bf16[256,1152]{1,0:T(8,128)(2,1)S(1)}, u32[]{:S(2)}) copy-start(bf16[256,1152]{1,0:T(8,128)(2,1)S(1)} %collective-permute-done.5.above_hbm) | copy-start | bytes 1769476
  32.3 8.0 %collective-permute-start.7 = (bf16[128,1152]{1,0:T(8,128)(2,1)S(1)}, bf16[128,1152]{1,0:T(8,128)(2,1)S(1)}, u32[]{:S(2)}, u32[]{:S(2)}) collective-permute-start(bf16[128,1152]{1,0:T(8,128)(2,1)S(1)} %slice.151), channel_id=1, source_target_pairs={{0,192},{16,56},{1,193},{17,57},{2,194},{18,58},{3,195},{19,59},{4... | collective-permute-start | bytes 884744 | tf_op jit(solution)/shard_map/ppermute | solution.py:59
  36.1 11.0 %copy-start.11 = (bf16[256,1152]{1,0:T(8,128)(2,1)}, bf16[256,1152]{1,0:T(8,128)(2,1)S(1)}, u32[]{:S(2)}) copy-start(bf16[256,1152]{1,0:T(8,128)(2,1)S(1)} %collective-permute-done.4.below_hbm) | copy-start | bytes 1769476
  36.1 8.0 %collective-permute-start.6 = (bf16[128,1152]{1,0:T(8,128)(2,1)S(1)}, bf16[128,1152]{1,0:T(8,128)(2,1)S(1)}, u32[]{:S(2)}, u32[]{:S(2)}) collective-permute-start(bf16[128,1152]{1,0:T(8,128)(2,1)S(1)} %slice.150), channel_id=1, source_target_pairs={{0,64},{16,48},{1,65},{17,49},{2,66},{18,50},{3,67},{19,51},{4,68}... | collective-permute-start | bytes 884744 | tf_op jit(solution)/shard_map/ppermute | solution.py:59
  40.4 6.7 %copy-start.12 = (bf16[128,1152]{1,0:T(8,128)(2,1)}, bf16[128,1152]{1,0:T(8,128)(2,1)S(1)}, u32[]{:S(2)}) copy-start(bf16[128,1152]{1,0:T(8,128)(2,1)S(1)} %collective-permute-done.7.far_high_hbm) | copy-start | bytes 884740
  44.2 3.0 %copy-start.13 = (bf16[128,1152]{1,0:T(8,128)(2,1)}, bf16[128,1152]{1,0:T(8,128)(2,1)S(1)}, u32[]{:S(2)}) copy-start(bf16[128,1152]{1,0:T(8,128)(2,1)S(1)} %collective-permute-done.6.far_low_hbm) | copy-start | bytes 884740
  44.2 3.0 %copy-start = (bf16[8,64,1024]{2,1,0:T(8,128)(2,1)}, bf16[8,64,1024]{2,1,0:T(8,128)(2,1)S(1)}, u32[]{:S(2)}) copy-start(bf16[8,64,1024]{2,1,0:T(8,128)(2,1)S(1)} %all-to-all-done) | copy-start | bytes 3145732
  44.2 2.9 %collective-permute-start.8 = (bf16[512,1024]{1,0:T(8,128)(2,1)S(1)}, bf16[512,1024]{1,0:T(8,128)(2,1)S(1)}, u32[]{:S(2)}, u32[]{:S(2)}) collective-permute-start(bf16[512,1024]{1,0:T(8,128)(2,1)S(1)} %bitcast.54), channel_id=1, source_target_pairs={{0,16},{16,0},{1,17},{17,1},{2,18},{18,2},{3,19},{19,3},{4,20},{20... | collective-permute-start | bytes 3145736 | tf_op jit(solution)/shard_map/ppermute | solution.py:59
  47.1 1.0 copy-start.3
  71.3 7.7 %collective-permute-start.9 = (bf16[7,2,64,1024]{3,2,1,0:T(8,128)(2,1)}, bf16[7,2,64,1024]{3,2,1,0:T(8,128)(2,1)}, u32[]{:S(2)}, u32[]{:S(2)}) collective-permute-start(bf16[7,2,64,1024]{3,2,1,0:T(8,128)(2,1)} %get-tuple-element.22), channel_id=1, source_target_pairs={{0,16},{16,0},{1,17},{17,1},{2,18},{18,2},{3,19},{19,3},{4,20},{20... | collective-permute-start | bytes 5505032 | tf_op jit(solution)/shard_map/ppermute | solution.py:59
  71.5 5.2 %collective-permute-start.10 = (bf16[2,64,1024]{2,1,0:T(8,128)(2,1)}, bf16[2,64,1024]{2,1,0:T(8,128)(2,1)S(1)}, u32[]{:S(2)}, u32[]{:S(2)}) collective-permute-start(bf16[2,64,1024]{2,1,0:T(8,128)(2,1)} %get-tuple-element.24), channel_id=1, source_target_pairs={{0,16},{16,0},{1,17},{17,1},{2,18},{18,2},{3,19},{19,3},{4,20},{20... | collective-permute-start | bytes 786440 | tf_op jit(solution)/shard_map/ppermute | solution.py:59
  71.9 4.9 %copy-start.9 = (bf16[2,64,1024]{2,1,0:T(8,128)(2,1)S(1)}, bf16[2,64,1024]{2,1,0:T(8,128)(2,1)}, u32[]{:S(2)}) copy-start(bf16[2,64,1024]{2,1,0:T(8,128)(2,1)} %get-tuple-element.23) | copy-start | bytes 786436
  71.9 7.1 %copy-start.7 = (bf16[7,2,64,1024]{3,2,1,0:T(8,128)(2,1)S(1)}, bf16[7,2,64,1024]{3,2,1,0:T(8,128)(2,1)}, u32[]{:S(2)}) copy-start(bf16[7,2,64,1024]{3,2,1,0:T(8,128)(2,1)} %get-tuple-element.21) | copy-start | bytes 5505028
  71.9 37.9 %all-to-all-start.1 = ((bf16[16,64,1024]{2,1,0:T(8,128)(2,1)}), bf16[16,64,1024]{2,1,0:T(8,128)(2,1)}, u32[]{:S(2)}, u32[]{:S(2)}) async-start(bf16[16,64,1024]{2,1,0:T(8,128)(2,1)} %bitcast.57), calls=%async_computation.1 | async-start | bytes 4194304 | tf_op jit(solution)/shard_map/all_to_all | solution.py:490
  76.9 7.3 %collective-permute-start.11 = (bf16[64,1024]{1,0:T(8,128)(2,1)S(1)}, bf16[64,1024]{1,0:T(8,128)(2,1)S(1)}, u32[]{:S(2)}, u32[]{:S(2)}) collective-permute-start(bf16[64,1024]{1,0:T(8,128)(2,1)S(1)} %get-tuple-element.39), channel_id=1, source_target_pairs={{0,1},{16,17},{1,2},{17,18},{2,3},{18,19},{3,4},{19,20},{4,5},{20,... | collective-permute-start | bytes 393224 | tf_op jit(solution)/shard_map/ppermute | solution.py:59
  78.4 5.0 %collective-permute-start.15 = (bf16[64,1024]{1,0:T(8,128)(2,1)S(1)}, bf16[64,1024]{1,0:T(8,128)(2,1)S(1)}, u32[]{:S(2)}, u32[]{:S(2)}) collective-permute-start(bf16[64,1024]{1,0:T(8,128)(2,1)S(1)} %get-tuple-element.40), channel_id=1, source_target_pairs={{0,7},{16,23},{1,0},{17,16},{2,1},{18,17},{3,2},{19,18},{4,3},{20,... | collective-permute-start | bytes 393224 | tf_op jit(solution)/shard_map/ppermute | solution.py:59
  83.5 8.1 %collective-permute-start.16 = (bf16[128,1024]{1,0:T(8,128)(2,1)S(1)}, bf16[128,1024]{1,0:T(8,128)(2,1)S(1)}, u32[]{:S(2)}, u32[]{:S(2)}) collective-permute-start(bf16[128,1024]{1,0:T(8,128)(2,1)S(1)} %pad_maximum_fusion.1), channel_id=1, source_target_pairs={{0,7},{16,23},{1,0},{17,16},{2,1},{18,17},{3,2},{19,18},{4,3},{20,... | collective-permute-start | bytes 786440 | tf_op jit(solution)/shard_map/ppermute | solution.py:59
  84.2 8.7 %collective-permute-start.12 = (bf16[128,1024]{1,0:T(8,128)(2,1)S(1)}, bf16[128,1024]{1,0:T(8,128)(2,1)S(1)}, u32[]{:S(2)}, u32[]{:S(2)}) collective-permute-start(bf16[128,1024]{1,0:T(8,128)(2,1)S(1)} %pad_maximum_fusion), channel_id=1, source_target_pairs={{0,1},{16,17},{1,2},{17,18},{2,3},{18,19},{3,4},{19,20},{4,5},{20,... | collective-permute-start | bytes 786440 | tf_op jit(solution)/shard_map/ppermute | solution.py:59
  91.6 7.4 %collective-permute-start.17 = (bf16[128,1024]{1,0:T(8,128)(2,1)S(1)}, bf16[128,1024]{1,0:T(8,128)(2,1)S(1)}, u32[]{:S(2)}, u32[]{:S(2)}) collective-permute-start(bf16[128,1024]{1,0:T(8,128)(2,1)S(1)} %fusion), channel_id=1, source_target_pairs={{0,7},{16,23},{1,0},{17,16},{2,1},{18,17},{3,2},{19,18},{4,3},{20,... | collective-permute-start | bytes 786440 | tf_op jit(solution)/shard_map/ppermute | solution.py:59
  93.0 16.9 %copy-start.1 = (bf16[8,64,1024]{2,1,0:T(8,128)(2,1)S(1)}, bf16[8,64,1024]{2,1,0:T(8,128)(2,1)}, u32[]{:S(2)}) copy-start(bf16[8,64,1024]{2,1,0:T(8,128)(2,1)} %copy-done) | copy-start | bytes 3145732
  93.0 16.9 %copy-start.4 = (bf16[512,1024]{1,0:T(8,128)(2,1)S(1)}, bf16[512,1024]{1,0:T(8,128)(2,1)}, u32[]{:S(2)}) copy-start(bf16[512,1024]{1,0:T(8,128)(2,1)} %copy-done.3) | copy-start | bytes 3145732
  93.0 16.9 %copy-start.6 = (f32[8,1024]{1,0:T(8,128)S(1)}, f32[8,1024]{1,0:T(8,128)}, u32[]{:S(2)}) copy-start(f32[8,1024]{1,0:T(8,128)} %get-tuple-element.27.loss_ref) | copy-start | bytes 98308
  93.0 7.6 %collective-permute-start.13 = (bf16[128,1024]{1,0:T(8,128)(2,1)S(1)}, bf16[128,1024]{1,0:T(8,128)(2,1)S(1)}, u32[]{:S(2)}, u32[]{:S(2)}) collective-permute-start(bf16[128,1024]{1,0:T(8,128)(2,1)S(1)} %fusion.2), channel_id=1, source_target_pairs={{0,1},{16,17},{1,2},{17,18},{2,3},{18,19},{3,4},{19,20},{4,5},{20,... | collective-permute-start | bytes 786440 | tf_op jit(solution)/shard_map/ppermute | solution.py:59
  99.0 7.2 %collective-permute-start.18 = (bf16[128,1024]{1,0:T(8,128)(2,1)S(1)}, bf16[128,1024]{1,0:T(8,128)(2,1)S(1)}, u32[]{:S(2)}, u32[]{:S(2)}) collective-permute-start(bf16[128,1024]{1,0:T(8,128)(2,1)S(1)} %fusion.1), channel_id=1, source_target_pairs={{0,7},{16,23},{1,0},{17,16},{2,1},{18,17},{3,2},{19,18},{4,3},{20,... | collective-permute-start | bytes 786440 | tf_op jit(solution)/shard_map/ppermute | solution.py:59
  100.8 7.9 %collective-permute-start.14 = (bf16[128,1024]{1,0:T(8,128)(2,1)S(1)}, bf16[128,1024]{1,0:T(8,128)(2,1)S(1)}, u32[]{:S(2)}, u32[]{:S(2)}) collective-permute-start(bf16[128,1024]{1,0:T(8,128)(2,1)S(1)} %fusion.3), channel_id=1, source_target_pairs={{0,1},{16,17},{1,2},{17,18},{2,3},{18,19},{3,4},{19,20},{4,5},{20,... | collective-permute-start | bytes 786440 | tf_op jit(solution)/shard_map/ppermute | solution.py:59
  111.2 17.0 %all-to-all-start.2 = ((bf16[16,144,128]{2,1,0:T(8,128)(2,1)}), bf16[16,144,128]{2,1,0:T(8,128)(2,1)S(1)}, u32[]{:S(2)}, u32[]{:S(2)}) async-start(bf16[16,144,128]{2,1,0:T(8,128)(2,1)} %shard_map.86), calls=%async_computation.2 | async-start | bytes 1179648 | tf_op jit(solution)/shard_map/all_to_all | solution.py:509
  129.1 23.4 %all-to-all-start.3 = ((bf16[16,112,128]{2,1,0:T(8,128)(2,1)}), bf16[16,112,128]{2,1,0:T(8,128)(2,1)S(1)}, u32[]{:S(2)}, u32[]{:S(2)}) async-start(bf16[16,112,128]{2,1,0:T(8,128)(2,1)} %shard_map.87), calls=%async_computation.3 | async-start | bytes 917504 | tf_op jit(solution)/shard_map/all_to_all | solution.py:518
  137.5 15.1 %copy-start.2 = (bf16[1024,1024]{1,0:T(8,128)(2,1)S(1)}, bf16[1024,1024]{1,0:T(8,128)(2,1)}, u32[]{:S(2)}) copy-start(bf16[1024,1024]{1,0:T(8,128)(2,1)} %head_ref.1) | copy-start | bytes 6291460

commit v2 on v1

--- a/solution.py
+++ b/solution.py
@@ -197,14 +197,14 @@
                     1 + len(pose_in),
                 )
             )
-    text_head_in = fetch(text_head_hbm, text_head_ref, 17)
-    own_in = fetch(text_own_hbm, text_feats_ref.at[half_rows(second), :], 18)
-    other_in = fetch(text_other_hbm, text_feats_ref.at[half_rows(1 - second), :], 19)
 
     pose_raws, text_raws = [], []
     pose_head_in.wait()
     for copy in pose_in:
         copy.wait()
+    text_head_in = fetch(text_head_hbm, text_head_ref, 17)
+    own_in = fetch(text_own_hbm, text_feats_ref.at[half_rows(second), :], 18)
+    other_in = fetch(text_other_hbm, text_feats_ref.at[half_rows(1 - second), :], 19)
     for step in range(STEPS):
         pose_raws.append(dot(pose_head_ref[...], pose_feats_ref[cols(step), :N], TT))
     text_head_in.wait()
@@ -269,13 +269,13 @@
     for step in range(STEPS):
         back = back_cols(pose_grads[step], pose_unit_ref[:, cols(step)], pose_inverses[step])
         pose_back_ref[:, cols(step)] = back
+        pose_rows_ref[cols(step), :] = pose_back_ref[:, cols(step)].T
+        store(pose_rows_ref.at[cols(step), :], pose_rows_hbm.at[cols(step), :])
     for step in range(STEPS):
         pose_term_ref[:, :, :, cols(step)] = split(
             dot(pose_back_ref[...], pose_feats_ref[:, cols(step)], NN)
         )
         store_halves(pose_term_ref, 1, cols(step))
-        pose_rows_ref[cols(step), :] = pose_back_ref[:, cols(step)].T
-        store(pose_rows_ref.at[cols(step), :], pose_rows_hbm.at[cols(step), :])
     for copy in out:
         copy.wait()
 

time: 155 us -> 155 us (level)
  no operation moved by 1% of the time
where the time goes in v2:
time: 155 us; the launch traced here: 154 us
  waiting for transfers between devices  60.9 us (39%)
  starting transfers between devices  52 us (34%)
  Pallas kernels  28.3 us (18%)
  other arithmetic  6.52 us (4%)
  matrix products  3.06 us (2%)
  local copies, waits for them, and re-layouts  2.53 us (2%)
    ppermute x19, waiting for transfers between devices, send(): return lax.ppermute(value, AXES, pairs_of(move))  39.6 us
    ppermute x19, starting transfers between devices, send(): return lax.ppermute(value, AXES, pairs_of(move))  24.1 us
    pallas_call x1, Pallas kernels, score(): pl.pallas_call(functools.partial(pair_kernel, scale, grad_scale), out_sha...  23.2 us
    all_to_all x1, waiting for transfers between devices, local(): plane = lax.all_to_all(terms, PLANE, 0, 0)  10.5 us
    all_to_all x1, waiting for transfers between devices, local(): line = lax.all_to_all(turned, LINE, 0, 0)  9.84 us
    all_to_all x1, starting transfers between devices, local(): line = lax.all_to_all(turned, LINE, 0, 0)  8.62 us
    all_to_all x1, starting transfers between devices, local(): text_own = lax.all_to_all(repeat(text_feats), 'z', 0, 0)  8.58 us
    all_to_all x1, starting transfers between devices, local(): plane = lax.all_to_all(terms, PLANE, 0, 0)  5.93 us
  transfers between devices with their start and end apart: 23, of which 15 were waited for; matrix products, arithmetic and copies ran while one was open for 5% of the time, Pallas kernels for 1%

profile of v2, /device:TPU:32, one launch (start us, length us, event | category | flops | bytes accessed | tf_op | source)
XLA Modules:
  0.0 154.3 jit_solution(13450917864597536680)
XLA Ops:
  0.7 0.7 convert_bitcast_fusion
  1.4 0.1 copy.14
  1.5 0.9 fusion.11
  2.5 1.7 %collective-permute-start = (bf16[64,1152]{1,0:T(8,128)(2,1)S(1)}, bf16[64,1152]{1,0:T(8,128)(2,1)S(1)}, u32[]{:S(2)}, u32[]{:S(2)}) collective-permute-start(bf16[64,1152]{1,0:T(8,128)(2,1)S(1)} %get-tuple-element.43), channel_id=1, source_target_pairs={{0,32},{16,80},{1,33},{17,81},{2,34},{18,82},{3,35},{19,83},{4,36}... | collective-permute-start | bytes 442376 | tf_op jit(solution)/shard_map/ppermute | solution.py:59
  4.1 1.7 %collective-permute-start.1 = (bf16[64,1152]{1,0:T(8,128)(2,1)S(1)}, bf16[64,1152]{1,0:T(8,128)(2,1)S(1)}, u32[]{:S(2)}, u32[]{:S(2)}) collective-permute-start(bf16[64,1152]{1,0:T(8,128)(2,1)S(1)} %get-tuple-element.43), channel_id=1, source_target_pairs={{0,40},{16,208},{1,41},{17,209},{2,42},{18,210},{3,43},{19,211},{4... | collective-permute-start | bytes 442376 | tf_op jit(solution)/shard_map/ppermute | solution.py:59
  5.8 0.9 copy-done.5
  6.7 1.1 shard_map.84
  7.8 8.6 %all-to-all-start = ((bf16[8,64,1024]{2,1,0:T(8,128)(2,1)}), bf16[8,64,1024]{2,1,0:T(8,128)(2,1)S(1)}, u32[]{:S(2)}, u32[]{:S(2)}) async-start(bf16[8,64,1024]{2,1,0:T(8,128)(2,1)} %shard_map.84), calls=%async_computation | async-start | bytes 2097152 | tf_op jit(solution)/shard_map/all_to_all | solution.py:473
  16.4 0.0 collective-permute-done
  16.4 0.4 collective-permute-start.2
  16.8 0.0 collective-permute-done.1
  16.8 2.9 %collective-permute-start.3 = (bf16[32,1152]{1,0:T(8,128)(2,1)S(1)}, bf16[32,1152]{1,0:T(8,128)(2,1)S(1)}, u32[]{:S(2)}, u32[]{:S(2)}) collective-permute-start(bf16[32,1152]{1,0:T(8,128)(2,1)S(1)} %slice.149), channel_id=1, source_target_pairs={{0,40},{16,208},{1,41},{17,209},{2,42},{18,210},{3,43},{19,211},{4... | collective-permute-start | bytes 221192 | tf_op jit(solution)/shard_map/ppermute | solution.py:59
  19.8 2.2 %collective-permute-done.2 = bf16[32,1152]{1,0:T(8,128)(2,1)S(1)} collective-permute-done((bf16[32,1152]{1,0:T(8,128)(2,1)S(1)}, bf16[32,1152]{1,0:T(8,128)(2,1)S(1)}, u32[]{:S(2)}, u32[]{:S(2)}) %collective-permute-start.2) | collective-permute-done | bytes 73760 | tf_op jit(solution)/shard_map/ppermute | solution.py:59
  22.0 0.0 collective-permute-done.3
  22.1 2.8 %collective-permute-start.5 = (bf16[256,1152]{1,0:T(8,128)(2,1)S(1)}, bf16[256,1152]{1,0:T(8,128)(2,1)S(1)}, u32[]{:S(2)}, u32[]{:S(2)}) collective-permute-start(bf16[256,1152]{1,0:T(8,128)(2,1)S(1)} %constant_dynamic-update-slice_fusion.near_hbm), channel_id=1, source_target_pairs={{0,192},{16,56},{1,193},{17,57},{2,194},{18,58},{3,195},{19,59},{4... | collective-permute-start | bytes 1769480 | tf_op jit(solution)/shard_map/ppermute | solution.py:59
  24.9 0.0 collective-permute-start.4
  24.9 7.4 %collective-permute-done.5.above_hbm = bf16[256,1152]{1,0:T(8,128)(2,1)S(1)} collective-permute-done((bf16[256,1152]{1,0:T(8,128)(2,1)S(1)}, bf16[256,1152]{1,0:T(8,128)(2,1)S(1)}, u32[]{:S(2)}, u32[]{:S(2)}) %collective-permute-start.5) | collective-permute-done | bytes 589856 | tf_op jit(solution)/shard_map/ppermute | solution.py:59
  32.3 3.8 %collective-permute-start.7 = (bf16[128,1152]{1,0:T(8,128)(2,1)S(1)}, bf16[128,1152]{1,0:T(8,128)(2,1)S(1)}, u32[]{:S(2)}, u32[]{:S(2)}) collective-permute-start(bf16[128,1152]{1,0:T(8,128)(2,1)S(1)} %slice.151), channel_id=1, source_target_pairs={{0,192},{16,56},{1,193},{17,57},{2,194},{18,58},{3,195},{19,59},{4... | collective-permute-start | bytes 884744 | tf_op jit(solution)/shard_map/ppermute | solution.py:59
  36.1 0.0 collective-permute-done.4.below_hbm
  36.1 0.1 collective-permute-start.6
  36.2 4.1 %collective-permute-done.7.far_high_hbm = bf16[128,1152]{1,0:T(8,128)(2,1)S(1)} collective-permute-done((bf16[128,1152]{1,0:T(8,128)(2,1)S(1)}, bf16[128,1152]{1,0:T(8,128)(2,1)S(1)}, u32[]{:S(2)}, u32[]{:S(2)}) %collective-permute-start.7) | collective-permute-done | bytes 294944 | tf_op jit(solution)/shard_map/ppermute | solution.py:59
  40.4 3.8 %collective-permute-done.6.far_low_hbm = bf16[128,1152]{1,0:T(8,128)(2,1)S(1)} collective-permute-done((bf16[128,1152]{1,0:T(8,128)(2,1)S(1)}, bf16[128,1152]{1,0:T(8,128)(2,1)S(1)}, u32[]{:S(2)}, u32[]{:S(2)}) %collective-permute-start.6) | collective-permute-done | bytes 294944 | tf_op jit(solution)/shard_map/ppermute | solution.py:59
  44.2 0.3 collective-permute-start.8
  44.4 2.6 %collective-permute-done.8.text_other_hbm.other_ref = bf16[512,1024]{1,0:T(8,128)(2,1)S(1)} collective-permute-done((bf16[512,1024]{1,0:T(8,128)(2,1)S(1)}, bf16[512,1024]{1,0:T(8,128)(2,1)S(1)}, u32[]{:S(2)}, u32[]{:S(2)}) %collective-permute-start.8) | collective-permute-done | bytes 1048608 | tf_op jit(solution)/shard_map/ppermute | solution.py:59
  47.1 1.0 copy-done.3
  48.1 23.2 %shard_map.85 = (f32[8,1024]{1,0:T(8,128)}, bf16[1024,1024]{1,0:T(8,128)(2,1)}, bf16[7,2,64,1024]{3,2,1,0:T(8,128)(2,1)}, bf16[7,2,64,1024]{3,2,1,0:T(8,128)(2,1...) custom-call(bf16[256,1152]{1,0:T(8,128)(2,1)} %copy-done.8, bf16[256,1152]{1,0:T(8,128)(2,1)} %copy-done.11, ...), custom_call_target="tpu_custom_call" | custom-call | flops 12884901888 | bytes 20971520 | tf_op jit(solution)/shard_map/pallas_call | solution.py:363
  71.3 0.2 collective-permute-start.9
  71.6 0.4 collective-permute-start.10
  71.9 4.9 %all-to-all-start.1 = ((bf16[16,64,1024]{2,1,0:T(8,128)(2,1)}), bf16[16,64,1024]{2,1,0:T(8,128)(2,1)}, u32[]{:S(2)}, u32[]{:S(2)}) async-start(bf16[16,64,1024]{2,1,0:T(8,128)(2,1)} %bitcast.57), calls=%async_computation.1 | async-start | bytes 4194304 | tf_op jit(solution)/shard_map/all_to_all | solution.py:490
  76.8 0.1 fusion.12
  76.9 1.5 collective-permute-start.11
  78.4 0.6 collective-permute-start.15
  79.0 2.1 %convert_add_fusion.3 = (f32[1,2,64,1024]{3,2,1,0:T(8,128)S(1)}, f32[1,2,64,1024]{3,2,1,0:T(8,128)S(1)}, f32[1,2,64,1024]{3,2,1,0:T(8,128)S(1)}, f32[1,2,64,1024...) fusion(bf16[7,2,64,1024]{3,2,1,0:T(8,128)(2,1)} %collective-per, ...), kind=kLoop, calls=%fused_computation.14 | loop fusion | flops 2752512 | bytes 7340032 | tf_op jit(solution)/shard_map/add | solution.py:426
  81.2 2.3 %collective-permute-done.15 = bf16[64,1024]{1,0:T(8,128)(2,1)S(1)} collective-permute-done((bf16[64,1024]{1,0:T(8,128)(2,1)S(1)}, bf16[64,1024]{1,0:T(8,128)(2,1)S(1)}, u32[]{:S(2)}, u32[]{:S(2)}) %collective-permute-start.15) | collective-permute-done | bytes 131104 | tf_op jit(solution)/shard_map/ppermute | solution.py:59
  83.5 0.7 collective-permute-start.16
  84.2 1.9 %collective-permute-start.12 = (bf16[128,1024]{1,0:T(8,128)(2,1)S(1)}, bf16[128,1024]{1,0:T(8,128)(2,1)S(1)}, u32[]{:S(2)}, u32[]{:S(2)}) collective-permute-start(bf16[128,1024]{1,0:T(8,128)(2,1)S(1)} %pad_maximum_fusion), channel_id=1, source_target_pairs={{0,1},{16,17},{1,2},{17,18},{2,3},{18,19},{3,4},{19,20},{4,5},{20,... | collective-permute-start | bytes 786440 | tf_op jit(solution)/shard_map/ppermute | solution.py:59
  86.2 5.4 %collective-permute-done.16 = bf16[128,1024]{1,0:T(8,128)(2,1)S(1)} collective-permute-done((bf16[128,1024]{1,0:T(8,128)(2,1)S(1)}, bf16[128,1024]{1,0:T(8,128)(2,1)S(1)}, u32[]{:S(2)}, u32[]{:S(2)}) %collective-permute-start.16) | collective-permute-done | bytes 262176 | tf_op jit(solution)/shard_map/ppermute | solution.py:59
  91.6 0.1 fusion
  91.6 0.9 collective-permute-start.17
  92.5 0.5 collective-permute-done.12
  93.0 0.1 fusion.2
  93.1 1.5 collective-permute-start.13
  94.6 4.4 %collective-permute-done.17 = bf16[128,1024]{1,0:T(8,128)(2,1)S(1)} collective-permute-done((bf16[128,1024]{1,0:T(8,128)(2,1)S(1)}, bf16[128,1024]{1,0:T(8,128)(2,1)S(1)}, u32[]{:S(2)}, u32[]{:S(2)}) %collective-permute-start.17) | collective-permute-done | bytes 262176 | tf_op jit(solution)/shard_map/ppermute | solution.py:59
  99.0 0.1 fusion.1
  99.1 1.2 collective-permute-start.18
  100.2 0.5 collective-permute-done.13
  100.7 0.1 fusion.3
  100.8 1.6 %collective-permute-start.14 = (bf16[128,1024]{1,0:T(8,128)(2,1)S(1)}, bf16[128,1024]{1,0:T(8,128)(2,1)S(1)}, u32[]{:S(2)}, u32[]{:S(2)}) collective-permute-start(bf16[128,1024]{1,0:T(8,128)(2,1)S(1)} %fusion.3), channel_id=1, source_target_pairs={{0,1},{16,17},{1,2},{17,18},{2,3},{18,19},{3,4},{19,20},{4,5},{20,... | collective-permute-start | bytes 786440 | tf_op jit(solution)/shard_map/ppermute | solution.py:59
  102.4 3.9 %collective-permute-done.18 = bf16[128,1024]{1,0:T(8,128)(2,1)S(1)} collective-permute-done((bf16[128,1024]{1,0:T(8,128)(2,1)S(1)}, bf16[128,1024]{1,0:T(8,128)(2,1)S(1)}, u32[]{:S(2)}, u32[]{:S(2)}) %collective-permute-start.18) | collective-permute-done | bytes 262176 | tf_op jit(solution)/shard_map/ppermute | solution.py:59
  106.3 2.4 %collective-permute-done.14 = bf16[128,1024]{1,0:T(8,128)(2,1)S(1)} collective-permute-done((bf16[128,1024]{1,0:T(8,128)(2,1)S(1)}, bf16[128,1024]{1,0:T(8,128)(2,1)S(1)}, u32[]{:S(2)}, u32[]{:S(2)}) %collective-permute-start.14) | collective-permute-done | bytes 262176 | tf_op jit(solution)/shard_map/ppermute | solution.py:59
  108.7 0.1 fusion.5.both_ref
  108.8 1.0 all-to-all-done.1
  109.8 1.3 shard_map.86
  111.1 5.9 %all-to-all-start.2 = ((bf16[16,144,128]{2,1,0:T(8,128)(2,1)}), bf16[16,144,128]{2,1,0:T(8,128)(2,1)S(1)}, u32[]{:S(2)}, u32[]{:S(2)}) async-start(bf16[16,144,128]{2,1,0:T(8,128)(2,1)} %shard_map.86), calls=%async_computation.2 | async-start | bytes 1179648 | tf_op jit(solution)/shard_map/all_to_all | solution.py:509
  117.1 0.2 reshape.87
  117.3 0.1 copy.17
  117.4 0.1 pad_maximum_fusion.2.rows_ref
  117.5 10.5 %all-to-all-done.2.plane_ref = bf16[16,144,128]{2,1,0:T(8,128)(2,1)S(1)} async-done(((bf16[16,144,128]{2,1,0:T(8,128)(2,1)}), bf16[16,144,128]{2,1,0:T(8,128)(2,1)S(1)}, u32[]{:S(2)}, u32[]{:S(2)}) %all-to-all-start.2) | async-done | bytes 589856 | tf_op jit(solution)/shard_map/all_to_all | solution.py:509
  128.0 0.9 shard_map.87
  128.9 8.6 %all-to-all-start.3 = ((bf16[16,112,128]{2,1,0:T(8,128)(2,1)}), bf16[16,112,128]{2,1,0:T(8,128)(2,1)S(1)}, u32[]{:S(2)}, u32[]{:S(2)}) async-start(bf16[16,112,128]{2,1,0:T(8,128)(2,1)} %shard_map.87), calls=%async_computation.3 | async-start | bytes 917504 | tf_op jit(solution)/shard_map/all_to_all | solution.py:518
  137.5 2.1 %reduce_sum.12 = bf16[64,1024]{1,0:T(8,128)(2,1)S(1)} reduce(bf16[16,64,1024]{2,1,0:T(8,128)(2,1)} %all-to-all-done.1, bf16[]{:T(256)} %constant.144.clone.1), dimensions={0}, to_apply=%region_0.1 | reduce | flops 983040 | bytes 2228226 | tf_op jit(solution)/shard_map/reduce_sum | solution.py:496
  139.7 3.1 %fusion.19 = f32[64,1024]{1,0:T(8,128)} fusion(bf16[64,1024]{1,0:T(8,128)(2,1)S(1)} %reduce_sum.12, bf16[1024,1024]{1,0:T(8,128)(2,1)} %pose_head_hbm.1), kind=kOutput, calls=%fused_computation.54 | convolution fusion | flops 134217728 | bytes 2490368 | tf_op jit(solution)/shard_map/dot_general | solution.py:90
  142.7 9.8 %all-to-all-done.3.line_ref = bf16[16,112,128]{2,1,0:T(8,128)(2,1)S(1)} async-done(((bf16[16,112,128]{2,1,0:T(8,128)(2,1)}), bf16[16,112,128]{2,1,0:T(8,128)(2,1)S(1)}, u32[]{:S(2)}, u32[]{:S(2)}) %all-to-all-start.3) | async-done | bytes 458784 | tf_op jit(solution)/shard_map/all_to_all | solution.py:518
  152.6 1.7 %shard_map.88 = (f32[64,1024]{1,0:T(8,128)}, f32[64,2048]{1,0:T(8,128)}, f32[1,1]{1,0:T(1,128)}) custom-call(bf16[16,112,128]{2,1,0:T(8,128)(2,1)S(1)} %all-to-all-done.3.line_ref, bf16[1024,1024]{1,0:T(8,128)(2,1)S(1)} %copy-done.2), custom_call_target="tpu_custom_call" | custom-call | flops 134217728 | bytes 4194304 | tf_op jit(solution)/shard_map/pallas_call | solution.py:400
  (48 shorter events, 0.4 us)
Async XLA Ops:
  2.5 13.9 %collective-permute-start = (bf16[64,1152]{1,0:T(8,128)(2,1)S(1)}, bf16[64,1152]{1,0:T(8,128)(2,1)S(1)}, u32[]{:S(2)}, u32[]{:S(2)}) collective-permute-start(bf16[64,1152]{1,0:T(8,128)(2,1)S(1)} %get-tuple-element.43), channel_id=1, source_target_pairs={{0,32},{16,80},{1,33},{17,81},{2,34},{18,82},{3,35},{19,83},{4,36}... | collective-permute-start | bytes 442376 | tf_op jit(solution)/shard_map/ppermute | solution.py:59
  4.1 12.7 %collective-permute-start.1 = (bf16[64,1152]{1,0:T(8,128)(2,1)S(1)}, bf16[64,1152]{1,0:T(8,128)(2,1)S(1)}, u32[]{:S(2)}, u32[]{:S(2)}) collective-permute-start(bf16[64,1152]{1,0:T(8,128)(2,1)S(1)} %get-tuple-element.43), channel_id=1, source_target_pairs={{0,40},{16,208},{1,41},{17,209},{2,42},{18,210},{3,43},{19,211},{4... | collective-permute-start | bytes 442376 | tf_op jit(solution)/shard_map/ppermute | solution.py:59
  5.8 0.9 copy-start.5
  7.8 36.4 %all-to-all-start = ((bf16[8,64,1024]{2,1,0:T(8,128)(2,1)}), bf16[8,64,1024]{2,1,0:T(8,128)(2,1)S(1)}, u32[]{:S(2)}, u32[]{:S(2)}) async-start(bf16[8,64,1024]{2,1,0:T(8,128)(2,1)} %shard_map.84), calls=%async_computation | async-start | bytes 2097152 | tf_op jit(solution)/shard_map/all_to_all | solution.py:473
  16.4 5.6 %collective-permute-start.2 = (bf16[32,1152]{1,0:T(8,128)(2,1)S(1)}, bf16[32,1152]{1,0:T(8,128)(2,1)S(1)}, u32[]{:S(2)}, u32[]{:S(2)}) collective-permute-start(bf16[32,1152]{1,0:T(8,128)(2,1)S(1)} %slice.148), channel_id=1, source_target_pairs={{0,32},{16,80},{1,33},{17,81},{2,34},{18,82},{3,35},{19,83},{4,36}... | collective-permute-start | bytes 221192 | tf_op jit(solution)/shard_map/ppermute | solution.py:59
  16.8 5.2 %collective-permute-start.3 = (bf16[32,1152]{1,0:T(8,128)(2,1)S(1)}, bf16[32,1152]{1,0:T(8,128)(2,1)S(1)}, u32[]{:S(2)}, u32[]{:S(2)}) collective-permute-start(bf16[32,1152]{1,0:T(8,128)(2,1)S(1)} %slice.149), channel_id=1, source_target_pairs={{0,40},{16,208},{1,41},{17,209},{2,42},{18,210},{3,43},{19,211},{4... | collective-permute-start | bytes 221192 | tf_op jit(solution)/shard_map/ppermute | solution.py:59
  22.1 25.0 %copy-start.8 = (bf16[256,1152]{1,0:T(8,128)(2,1)}, bf16[256,1152]{1,0:T(8,128)(2,1)S(1)}, u32[]{:S(2)}) copy-start(bf16[256,1152]{1,0:T(8,128)(2,1)S(1)} %constant_dynamic-update-slice_fusion.near_hbm) | copy-start | bytes 1769476
  22.1 10.2 %collective-permute-start.5 = (bf16[256,1152]{1,0:T(8,128)(2,1)S(1)}, bf16[256,1152]{1,0:T(8,128)(2,1)S(1)}, u32[]{:S(2)}, u32[]{:S(2)}) collective-permute-start(bf16[256,1152]{1,0:T(8,128)(2,1)S(1)} %constant_dynamic-update-slice_fusion.near_hbm), channel_id=1, source_target_pairs={{0,192},{16,56},{1,193},{17,57},{2,194},{18,58},{3,195},{19,59},{4... | collective-permute-start | bytes 1769480 | tf_op jit(solution)/shard_map/ppermute | solution.py:59
  24.9 11.2 %collective-permute-start.4 = (bf16[256,1152]{1,0:T(8,128)(2,1)S(1)}, bf16[256,1152]{1,0:T(8,128)(2,1)S(1)}, u32[]{:S(2)}, u32[]{:S(2)}) collective-permute-start(bf16[256,1152]{1,0:T(8,128)(2,1)S(1)} %constant_dynamic-update-slice_fusion.near_hbm), channel_id=1, source_target_pairs={{0,64},{16,48},{1,65},{17,49},{2,66},{18,50},{3,67},{19,51},{4,68}... | collective-permute-start | bytes 1769480 | tf_op jit(solution)/shard_map/ppermute | solution.py:59
  32.3 14.8 %copy-start.10 = (bf16[256,1152]{1,0:T(8,128)(2,1)}, bf16[256,1152]{1,0:T(8,128)(2,1)S(1)}, u32[]{:S(2)}) copy-start(bf16[256,1152]{1,0:T(8,128)(2,1)S(1)} %collective-permute-done.5.above_hbm) | copy-start | bytes 1769476
  32.3 8.0 %collective-permute-start.7 = (bf16[128,1152]{1,0:T(8,128)(2,1)S(1)}, bf16[128,1152]{1,0:T(8,128)(2,1)S(1)}, u32[]{:S(2)}, u32[]{:S(2)}) collective-permute-start(bf16[128,1152]{1,0:T(8,128)(2,1)S(1)} %slice.151), channel_id=1, source_target_pairs={{0,192},{16,56},{1,193},{17,57},{2,194},{18,58},{3,195},{19,59},{4... | collective-permute-start | bytes 884744 | tf_op jit(solution)/shard_map/ppermute | solution.py:59
  36.1 11.0 %copy-start.11 = (bf16[256,1152]{1,0:T(8,128)(2,1)}, bf16[256,1152]{1,0:T(8,128)(2,1)S(1)}, u32[]{:S(2)}) copy-start(bf16[256,1152]{1,0:T(8,128)(2,1)S(1)} %collective-permute-done.4.below_hbm) | copy-start | bytes 1769476
  36.1 8.0 %collective-permute-start.6 = (bf16[128,1152]{1,0:T(8,128)(2,1)S(1)}, bf16[128,1152]{1,0:T(8,128)(2,1)S(1)}, u32[]{:S(2)}, u32[]{:S(2)}) collective-permute-start(bf16[128,1152]{1,0:T(8,128)(2,1)S(1)} %slice.150), channel_id=1, source_target_pairs={{0,64},{16,48},{1,65},{17,49},{2,66},{18,50},{3,67},{19,51},{4,68}... | collective-permute-start | bytes 884744 | tf_op jit(solution)/shard_map/ppermute | solution.py:59
  40.4 6.7 %copy-start.12 = (bf16[128,1152]{1,0:T(8,128)(2,1)}, bf16[128,1152]{1,0:T(8,128)(2,1)S(1)}, u32[]{:S(2)}) copy-start(bf16[128,1152]{1,0:T(8,128)(2,1)S(1)} %collective-permute-done.7.far_high_hbm) | copy-start | bytes 884740
  44.2 3.0 %copy-start.13 = (bf16[128,1152]{1,0:T(8,128)(2,1)}, bf16[128,1152]{1,0:T(8,128)(2,1)S(1)}, u32[]{:S(2)}) copy-start(bf16[128,1152]{1,0:T(8,128)(2,1)S(1)} %collective-permute-done.6.far_low_hbm) | copy-start | bytes 884740
  44.2 3.0 %copy-start = (bf16[8,64,1024]{2,1,0:T(8,128)(2,1)}, bf16[8,64,1024]{2,1,0:T(8,128)(2,1)S(1)}, u32[]{:S(2)}) copy-start(bf16[8,64,1024]{2,1,0:T(8,128)(2,1)S(1)} %all-to-all-done) | copy-start | bytes 3145732
  44.2 2.9 %collective-permute-start.8 = (bf16[512,1024]{1,0:T(8,128)(2,1)S(1)}, bf16[512,1024]{1,0:T(8,128)(2,1)S(1)}, u32[]{:S(2)}, u32[]{:S(2)}) collective-permute-start(bf16[512,1024]{1,0:T(8,128)(2,1)S(1)} %bitcast.54), channel_id=1, source_target_pairs={{0,16},{16,0},{1,17},{17,1},{2,18},{18,2},{3,19},{19,3},{4,20},{20... | collective-permute-start | bytes 3145736 | tf_op jit(solution)/shard_map/ppermute | solution.py:59
  47.1 1.0 copy-start.3
  71.3 7.7 %collective-permute-start.9 = (bf16[7,2,64,1024]{3,2,1,0:T(8,128)(2,1)}, bf16[7,2,64,1024]{3,2,1,0:T(8,128)(2,1)}, u32[]{:S(2)}, u32[]{:S(2)}) collective-permute-start(bf16[7,2,64,1024]{3,2,1,0:T(8,128)(2,1)} %get-tuple-element.22), channel_id=1, source_target_pairs={{0,16},{16,0},{1,17},{17,1},{2,18},{18,2},{3,19},{19,3},{4,20},{20... | collective-permute-start | bytes 5505032 | tf_op jit(solution)/shard_map/ppermute | solution.py:59
  71.6 5.2 %collective-permute-start.10 = (bf16[2,64,1024]{2,1,0:T(8,128)(2,1)}, bf16[2,64,1024]{2,1,0:T(8,128)(2,1)S(1)}, u32[]{:S(2)}, u32[]{:S(2)}) collective-permute-start(bf16[2,64,1024]{2,1,0:T(8,128)(2,1)} %get-tuple-element.24), channel_id=1, source_target_pairs={{0,16},{16,0},{1,17},{17,1},{2,18},{18,2},{3,19},{19,3},{4,20},{20... | collective-permute-start | bytes 786440 | tf_op jit(solution)/shard_map/ppermute | solution.py:59
  71.9 4.9 %copy-start.9 = (bf16[2,64,1024]{2,1,0:T(8,128)(2,1)S(1)}, bf16[2,64,1024]{2,1,0:T(8,128)(2,1)}, u32[]{:S(2)}) copy-start(bf16[2,64,1024]{2,1,0:T(8,128)(2,1)} %get-tuple-element.23) | copy-start | bytes 786436
  71.9 7.1 %copy-start.7 = (bf16[7,2,64,1024]{3,2,1,0:T(8,128)(2,1)S(1)}, bf16[7,2,64,1024]{3,2,1,0:T(8,128)(2,1)}, u32[]{:S(2)}) copy-start(bf16[7,2,64,1024]{3,2,1,0:T(8,128)(2,1)} %get-tuple-element.21) | copy-start | bytes 5505028
  71.9 37.9 %all-to-all-start.1 = ((bf16[16,64,1024]{2,1,0:T(8,128)(2,1)}), bf16[16,64,1024]{2,1,0:T(8,128)(2,1)}, u32[]{:S(2)}, u32[]{:S(2)}) async-start(bf16[16,64,1024]{2,1,0:T(8,128)(2,1)} %bitcast.57), calls=%async_computation.1 | async-start | bytes 4194304 | tf_op jit(solution)/shard_map/all_to_all | solution.py:490
  76.9 7.3 %collective-permute-start.11 = (bf16[64,1024]{1,0:T(8,128)(2,1)S(1)}, bf16[64,1024]{1,0:T(8,128)(2,1)S(1)}, u32[]{:S(2)}, u32[]{:S(2)}) collective-permute-start(bf16[64,1024]{1,0:T(8,128)(2,1)S(1)} %get-tuple-element.39), channel_id=1, source_target_pairs={{0,1},{16,17},{1,2},{17,18},{2,3},{18,19},{3,4},{19,20},{4,5},{20,... | collective-permute-start | bytes 393224 | tf_op jit(solution)/shard_map/ppermute | solution.py:59
  78.4 5.0 %collective-permute-start.15 = (bf16[64,1024]{1,0:T(8,128)(2,1)S(1)}, bf16[64,1024]{1,0:T(8,128)(2,1)S(1)}, u32[]{:S(2)}, u32[]{:S(2)}) collective-permute-start(bf16[64,1024]{1,0:T(8,128)(2,1)S(1)} %get-tuple-element.40), channel_id=1, source_target_pairs={{0,7},{16,23},{1,0},{17,16},{2,1},{18,17},{3,2},{19,18},{4,3},{20,... | collective-permute-start | bytes 393224 | tf_op jit(solution)/shard_map/ppermute | solution.py:59
  83.5 8.0 %collective-permute-start.16 = (bf16[128,1024]{1,0:T(8,128)(2,1)S(1)}, bf16[128,1024]{1,0:T(8,128)(2,1)S(1)}, u32[]{:S(2)}, u32[]{:S(2)}) collective-permute-start(bf16[128,1024]{1,0:T(8,128)(2,1)S(1)} %pad_maximum_fusion.1), channel_id=1, source_target_pairs={{0,7},{16,23},{1,0},{17,16},{2,1},{18,17},{3,2},{19,18},{4,3},{20,... | collective-permute-start | bytes 786440 | tf_op jit(solution)/shard_map/ppermute | solution.py:59
  84.2 8.7 %collective-permute-start.12 = (bf16[128,1024]{1,0:T(8,128)(2,1)S(1)}, bf16[128,1024]{1,0:T(8,128)(2,1)S(1)}, u32[]{:S(2)}, u32[]{:S(2)}) collective-permute-start(bf16[128,1024]{1,0:T(8,128)(2,1)S(1)} %pad_maximum_fusion), channel_id=1, source_target_pairs={{0,1},{16,17},{1,2},{17,18},{2,3},{18,19},{3,4},{19,20},{4,5},{20,... | collective-permute-start | bytes 786440 | tf_op jit(solution)/shard_map/ppermute | solution.py:59
  91.6 7.4 %collective-permute-start.17 = (bf16[128,1024]{1,0:T(8,128)(2,1)S(1)}, bf16[128,1024]{1,0:T(8,128)(2,1)S(1)}, u32[]{:S(2)}, u32[]{:S(2)}) collective-permute-start(bf16[128,1024]{1,0:T(8,128)(2,1)S(1)} %fusion), channel_id=1, source_target_pairs={{0,7},{16,23},{1,0},{17,16},{2,1},{18,17},{3,2},{19,18},{4,3},{20,... | collective-permute-start | bytes 786440 | tf_op jit(solution)/shard_map/ppermute | solution.py:59
  93.0 16.8 %copy-start.1 = (bf16[8,64,1024]{2,1,0:T(8,128)(2,1)S(1)}, bf16[8,64,1024]{2,1,0:T(8,128)(2,1)}, u32[]{:S(2)}) copy-start(bf16[8,64,1024]{2,1,0:T(8,128)(2,1)} %copy-done) | copy-start | bytes 3145732
  93.0 16.8 %copy-start.4 = (bf16[512,1024]{1,0:T(8,128)(2,1)S(1)}, bf16[512,1024]{1,0:T(8,128)(2,1)}, u32[]{:S(2)}) copy-start(bf16[512,1024]{1,0:T(8,128)(2,1)} %copy-done.3) | copy-start | bytes 3145732
  93.0 16.8 %copy-start.6 = (f32[8,1024]{1,0:T(8,128)S(1)}, f32[8,1024]{1,0:T(8,128)}, u32[]{:S(2)}) copy-start(f32[8,1024]{1,0:T(8,128)} %get-tuple-element.27.loss_ref) | copy-start | bytes 98308
  93.1 7.6 %collective-permute-start.13 = (bf16[128,1024]{1,0:T(8,128)(2,1)S(1)}, bf16[128,1024]{1,0:T(8,128)(2,1)S(1)}, u32[]{:S(2)}, u32[]{:S(2)}) collective-permute-start(bf16[128,1024]{1,0:T(8,128)(2,1)S(1)} %fusion.2), channel_id=1, source_target_pairs={{0,1},{16,17},{1,2},{17,18},{2,3},{18,19},{3,4},{19,20},{4,5},{20,... | collective-permute-start | bytes 786440 | tf_op jit(solution)/shard_map/ppermute | solution.py:59
  99.1 7.2 %collective-permute-start.18 = (bf16[128,1024]{1,0:T(8,128)(2,1)S(1)}, bf16[128,1024]{1,0:T(8,128)(2,1)S(1)}, u32[]{:S(2)}, u32[]{:S(2)}) collective-permute-start(bf16[128,1024]{1,0:T(8,128)(2,1)S(1)} %fusion.1), channel_id=1, source_target_pairs={{0,7},{16,23},{1,0},{17,16},{2,1},{18,17},{3,2},{19,18},{4,3},{20,... | collective-permute-start | bytes 786440 | tf_op jit(solution)/shard_map/ppermute | solution.py:59
  100.8 7.9 %collective-permute-start.14 = (bf16[128,1024]{1,0:T(8,128)(2,1)S(1)}, bf16[128,1024]{1,0:T(8,128)(2,1)S(1)}, u32[]{:S(2)}, u32[]{:S(2)}) collective-permute-start(bf16[128,1024]{1,0:T(8,128)(2,1)S(1)} %fusion.3), channel_id=1, source_target_pairs={{0,1},{16,17},{1,2},{17,18},{2,3},{18,19},{3,4},{19,20},{4,5},{20,... | collective-permute-start | bytes 786440 | tf_op jit(solution)/shard_map/ppermute | solution.py:59
  111.1 16.9 %all-to-all-start.2 = ((bf16[16,144,128]{2,1,0:T(8,128)(2,1)}), bf16[16,144,128]{2,1,0:T(8,128)(2,1)S(1)}, u32[]{:S(2)}, u32[]{:S(2)}) async-start(bf16[16,144,128]{2,1,0:T(8,128)(2,1)} %shard_map.86), calls=%async_computation.2 | async-start | bytes 1179648 | tf_op jit(solution)/shard_map/all_to_all | solution.py:509
  128.9 23.7 %all-to-all-start.3 = ((bf16[16,112,128]{2,1,0:T(8,128)(2,1)}), bf16[16,112,128]{2,1,0:T(8,128)(2,1)S(1)}, u32[]{:S(2)}, u32[]{:S(2)}) async-start(bf16[16,112,128]{2,1,0:T(8,128)(2,1)} %shard_map.87), calls=%async_computation.3 | async-start | bytes 917504 | tf_op jit(solution)/shard_map/all_to_all | solution.py:518
  137.5 15.1 %copy-start.2 = (bf16[1024,1024]{1,0:T(8,128)(2,1)S(1)}, bf16[1024,1024]{1,0:T(8,128)(2,1)}, u32[]{:S(2)}) copy-start(bf16[1024,1024]{1,0:T(8,128)(2,1)} %head_ref.1) | copy-start | bytes 6291460
